TPU v7x, 32 devices: a whole 2x2x4 slice. The times are simulated.
32 devices in a mesh: dp: 8 (over y, x, core), seq: 4 (over z).
Axes of the slice: x: 2, y: 2, z: 4, core: 2. Of those that a mesh axis runs over, the one named last changes fastest.
Arguments:
- inputs: bfloat16 [8, 512, 2048], P('dp', 'seq'), may hold values from -6 to 6
- cotangent: bfloat16 [8, 512, 2048], P('dp', 'seq'), may hold values from -6 to 6
- segments: int32 [8, 512], P('dp', 'seq'), may hold values from 0 to 16, as said below
- labels: int32 [8, 512], P('dp', 'seq'), may hold values from 0 to 1
- step_ends: int32 [8, 512], P('dp', 'seq'), may hold values 0 or 1
- attend_gain: bfloat16 [2048], P(('dp', 'seq')), may hold values from 0.5 to 1.5
- attend_shift: bfloat16 [2048], P(('dp', 'seq')), may hold values from -1 to 1
- project_in: bfloat16 [2048, 6144], P(('dp', 'seq')), may hold values from -0.1875 to 0.1875
- project_bias: bfloat16 [4096], P(('dp', 'seq')), may hold values from -1 to 1
- project_out: bfloat16 [2048, 2048], P(('dp', 'seq')), may hold values from -1 to 1
- output_bias: bfloat16 [2048], P(('dp', 'seq')), may hold values from -1 to 1
- dense_gain: bfloat16 [2048], P(('dp', 'seq')), may hold values from 0.5 to 1.5
- dense_shift: bfloat16 [2048], P(('dp', 'seq')), may hold values from -1 to 1
- up_weight: bfloat16 [2048, 8192], P(('dp', 'seq')), may hold values from -0.125 to 0.125
- up_bias: bfloat16 [8192], P(('dp', 'seq')), may hold values from -1 to 1
- down_weight: bfloat16 [8192, 2048], P(('dp', 'seq')), may hold values from -0.0625 to 0.0625
- down_bias: bfloat16 [2048], P(('dp', 'seq')), may hold values from -1 to 1
- reward_weight: bfloat16 [2048], P(('dp', 'seq')), may hold values from -0.125 to 0.125
Outputs:
- outputs: bfloat16 [8, 512, 2048], P('dp', 'seq')
- rewards: float32 [8, 512], P('dp', 'seq')
- inputs_gradient: float32 [8, 512, 2048], P('dp', 'seq')
- attend_gain_gradient: float32 [2048], P(('dp', 'seq'))
- attend_shift_gradient: float32 [2048], P(('dp', 'seq'))
- project_in_gradient: float32 [2048, 6144], P(('dp', 'seq'))
- project_bias_gradient: float32 [4096], P(('dp', 'seq'))
- project_out_gradient: float32 [2048, 2048], P(('dp', 'seq'))
- output_bias_gradient: float32 [2048], P(('dp', 'seq'))
- dense_gain_gradient: float32 [2048], P(('dp', 'seq'))
- dense_shift_gradient: float32 [2048], P(('dp', 'seq'))
- up_weight_gradient: float32 [2048, 8192], P(('dp', 'seq'))
- up_bias_gradient: float32 [8192], P(('dp', 'seq'))
- down_weight_gradient: float32 [8192, 2048], P(('dp', 'seq'))
- down_bias_gradient: float32 [2048], P(('dp', 'seq'))
- reward_weight_gradient: float32 [2048], P(('dp', 'seq'))
Inputs may be any that keep to these rules, and one draw needn't show every extreme that they name: `segments`: in each row, the positions before a prefix length of 64 to 128 hold 0; then come 4 to 16 solutions numbered 1 upward in order, each a run of one or more positions; one row has 16 solutions.
All inputs are finite; a program needn't handle non-finite values. No bound on the sum of `step_ends` on one device may be relied on, other than what follows from the above.
Results may differ from a plain program's by a relative error of at most 0.013.
Values may be sent and summed in bfloat16 or wider, within the bound.
No kernel may reach another device: no remote copies, remote signals or barrier semaphores. Data moves between devices by JAX's collectives and lax.ppermute only.
A program may use at most 272 MiB of HBM per device.

v0:
```python
from functools import partial

import jax
import jax.numpy as jnp
from jax import lax
from jax.sharding import PartitionSpec as P

HEADS = 16


EPSILON = 1e-05
MASKED = -1e30


def product(left, right):
    return jnp.dot(left, right, preferred_element_type=jnp.float32)


def inner_rows(left, right):
    return jnp.einsum("ta,tb->ab", left, right, preferred_element_type=jnp.float32)


def against_rows(left, right):
    return jnp.einsum("tb,ab->ta", left, right, preferred_element_type=jnp.float32)


def normalize_parts(field, gain, shift):
    center = field - jnp.mean(field, axis=-1, keepdims=True)
    spread = jnp.mean(center * center, axis=-1, keepdims=True)
    inverse = lax.rsqrt(spread + EPSILON)
    normal = center * inverse
    return (normal * gain + shift, normal, inverse)


def normalize_back(upstream, normal, inverse, gain):
    scaled = upstream * gain
    mean_scaled = jnp.mean(scaled, axis=-1, keepdims=True)
    mean_cross = jnp.mean(scaled * normal, axis=-1, keepdims=True)
    return inverse * (scaled - mean_scaled - normal * mean_cross)


def head_scores(query_heads, key_heads, allowed, score_scale):
    scores = (
        jnp.einsum("qhd,khd->hqk", query_heads, key_heads, preferred_element_type=jnp.float32)
        * score_scale
    )
    return jnp.where(allowed[None], scores, MASKED)


def visible(seg_query, seg_key, query_place, key_place):
    same_group = (seg_key[None, :] == 0) | (seg_key[None, :] == seg_query[:, None])
    return same_group & (key_place[None, :] <= query_place[:, None])


def forward_heads(query_heads, key_heads, value_heads, allowed, score_scale):
    scores = head_scores(query_heads, key_heads, allowed, score_scale)
    highest = jnp.max(scores, axis=-1, keepdims=True)
    exponent = jnp.exp(scores - highest)
    totals = jnp.sum(exponent, axis=-1, keepdims=True)
    chances_low = (exponent / totals).astype(jnp.bfloat16)
    mixture = jnp.einsum(
        "hqk,khd->qhd", chances_low, value_heads, preferred_element_type=jnp.float32
    )
    return (mixture, (highest + jnp.log(totals))[..., 0])


def backward_heads(query_heads, key_heads, value_heads, allowed, log_row, grad_heads, score_scale):
    scores = head_scores(query_heads, key_heads, allowed, score_scale)
    chances = jnp.exp(scores - log_row[..., None])
    chance_grad = jnp.einsum(
        "qhd,khd->hqk", grad_heads, value_heads, preferred_element_type=jnp.float32
    )
    weighted = jnp.sum(chances * chance_grad, axis=-1, keepdims=True)
    score_grad = (chances * (chance_grad - weighted)).astype(jnp.bfloat16)
    query_grad = (
        jnp.einsum("hqk,khd->qhd", score_grad, key_heads, preferred_element_type=jnp.float32)
        * score_scale
    )
    key_grad = (
        jnp.einsum("hqk,qhd->khd", score_grad, query_heads, preferred_element_type=jnp.float32)
        * score_scale
    )
    value_grad = jnp.einsum(
        "hqk,qhd->khd", chances.astype(jnp.bfloat16), grad_heads, preferred_element_type=jnp.float32
    )
    return (query_grad, key_grad, value_grad)


def spread_path(arguments):
    (
        inputs,
        cotangent,
        segments,
        labels,
        step_ends,
        attend_gain,
        attend_shift,
        project_in,
        project_bias,
        project_out,
        output_bias,
        dense_gain,
        dense_shift,
        up_weight,
        up_bias,
        down_weight,
        down_bias,
        reward_weight,
    ) = arguments
    rows_here, places_here, width = inputs.shape
    tokens_here = rows_here * places_here
    all_rows = rows_here * lax.axis_size("dp")
    head_width = width // HEADS
    score_scale = head_width ** (-0.5)
    attend_set = (
        lax.all_gather(attend_gain, ("dp", "seq"), axis=0, tiled=True),
        lax.all_gather(attend_shift, ("dp", "seq"), axis=0, tiled=True),
        lax.all_gather(project_in, ("dp", "seq"), axis=0, tiled=True),
        lax.all_gather(project_bias, ("dp", "seq"), axis=0, tiled=True),
        lax.all_gather(project_out, ("dp", "seq"), axis=0, tiled=True),
        lax.all_gather(output_bias, ("dp", "seq"), axis=0, tiled=True),
    )
    gain_one, shift_one, weight_in, bias_in, weight_out, bias_out = attend_set
    flat_inputs = inputs.reshape(tokens_here, width).astype(jnp.float32)
    first_value, first_normal, first_inverse = normalize_parts(
        flat_inputs, gain_one.astype(jnp.float32), shift_one.astype(jnp.float32)
    )
    first_low = first_value.astype(jnp.bfloat16)
    bias_wide = bias_in.astype(jnp.float32)
    bias_full = jnp.concatenate(
        [bias_wide[:width], jnp.zeros((width,), jnp.float32), bias_wide[width:]]
    )
    shifted = product(first_low, weight_in) + bias_full
    queries = shifted[:, :width].astype(jnp.bfloat16)
    keys_values = shifted[:, width:].astype(jnp.bfloat16).reshape(rows_here, places_here, 2 * width)
    query_rows = queries.reshape(rows_here, places_here, width)
    keys_all, segments_all = (
        lax.all_gather(keys_values, "seq", axis=1, tiled=True),
        lax.all_gather(segments, "seq", axis=1, tiled=True),
    )
    length = segments_all.shape[1]
    key_place = jnp.arange(length)
    query_place = lax.axis_index("seq") * places_here + jnp.arange(places_here)

    def split_heads(block):
        return block.reshape(block.shape[0], HEADS, head_width)

    def attend_forward(bundle):
        query_row, pairs_row, seg_query, seg_key = bundle
        mixture, log_row = forward_heads(
            split_heads(query_row),
            split_heads(pairs_row[:, :width]),
            split_heads(pairs_row[:, width:]),
            visible(seg_query, seg_key, query_place, key_place),
            score_scale,
        )
        return (mixture.reshape(places_here, width), log_row)

    mixture_rows, log_totals = lax.map(
        attend_forward, (query_rows, keys_all, segments, segments_all)
    )
    mixture_low = mixture_rows.reshape(tokens_here, width).astype(jnp.bfloat16)
    hidden = flat_inputs + product(mixture_low, weight_out) + bias_out.astype(jnp.float32)
    dense_set = (
        lax.all_gather(dense_gain, ("dp", "seq"), axis=0, tiled=True),
        lax.all_gather(dense_shift, ("dp", "seq"), axis=0, tiled=True),
        lax.all_gather(up_weight, ("dp", "seq"), axis=0, tiled=True),
        lax.all_gather(up_bias, ("dp", "seq"), axis=0, tiled=True),
        lax.all_gather(down_weight, ("dp", "seq"), axis=0, tiled=True),
        lax.all_gather(down_bias, ("dp", "seq"), axis=0, tiled=True),
        lax.all_gather(reward_weight, ("dp", "seq"), axis=0, tiled=True),
    )
    gain_two, shift_two, weight_up, bias_up, weight_down, bias_down, reward_full = dense_set
    second_value, second_normal, second_inverse = normalize_parts(
        hidden, gain_two.astype(jnp.float32), shift_two.astype(jnp.float32)
    )
    second_low = second_value.astype(jnp.bfloat16)
    upward = product(second_low, weight_up) + bias_up.astype(jnp.float32)
    activated = jax.nn.gelu(upward, approximate=True).astype(jnp.bfloat16)
    result = hidden + product(activated, weight_down) + bias_down.astype(jnp.float32)
    reward_wide = reward_full.astype(jnp.float32)
    rewards = jnp.sum(result * reward_wide, axis=-1)
    scored = (step_ends.reshape(tokens_here) * (segments.reshape(tokens_here) > 0)).astype(
        jnp.float32
    )
    targets = labels.reshape(tokens_here).astype(jnp.float32)
    error = scored * (jax.nn.sigmoid(rewards) - targets) / all_rows
    result_grad = (
        cotangent.reshape(tokens_here, width).astype(jnp.float32) + error[:, None] * reward_wide
    )
    reward_weight_gradient = jnp.sum(error[:, None] * result, axis=0)
    dense_back = (
        lax.all_gather(dense_gain, ("dp", "seq"), axis=0, tiled=True),
        lax.all_gather(dense_shift, ("dp", "seq"), axis=0, tiled=True),
        lax.all_gather(up_weight, ("dp", "seq"), axis=0, tiled=True),
        lax.all_gather(up_bias, ("dp", "seq"), axis=0, tiled=True),
        lax.all_gather(down_weight, ("dp", "seq"), axis=0, tiled=True),
        lax.all_gather(down_bias, ("dp", "seq"), axis=0, tiled=True),
        lax.all_gather(reward_weight, ("dp", "seq"), axis=0, tiled=True),
    )
    dense_low = result_grad.astype(jnp.bfloat16)
    down_weight_gradient = inner_rows(activated, dense_low)
    down_bias_gradient = jnp.sum(dense_low.astype(jnp.float32), axis=0)
    activated_grad = against_rows(dense_low, dense_back[4])
    gelu_value, gelu_pull = jax.vjp(partial(jax.nn.gelu, approximate=True), upward)
    upward_low = gelu_pull(activated_grad)[0].astype(jnp.bfloat16)
    up_weight_gradient = inner_rows(second_low, upward_low)
    up_bias_gradient = jnp.sum(upward_low.astype(jnp.float32), axis=0)
    second_grad = against_rows(upward_low, dense_back[2])
    dense_gain_gradient = jnp.sum(second_grad * second_normal, axis=0)
    dense_shift_gradient = jnp.sum(second_grad, axis=0)
    hidden_grad = result_grad + normalize_back(
        second_grad, second_normal, second_inverse, dense_back[0].astype(jnp.float32)
    )
    dense_sums = (
        lax.psum_scatter(dense_gain_gradient, ("dp", "seq"), scatter_dimension=0, tiled=True),
        lax.psum_scatter(dense_shift_gradient, ("dp", "seq"), scatter_dimension=0, tiled=True),
        lax.psum_scatter(up_weight_gradient, ("dp", "seq"), scatter_dimension=0, tiled=True),
        lax.psum_scatter(up_bias_gradient, ("dp", "seq"), scatter_dimension=0, tiled=True),
        lax.psum_scatter(down_weight_gradient, ("dp", "seq"), scatter_dimension=0, tiled=True),
        lax.psum_scatter(down_bias_gradient, ("dp", "seq"), scatter_dimension=0, tiled=True),
        lax.psum_scatter(reward_weight_gradient, ("dp", "seq"), scatter_dimension=0, tiled=True),
    )
    attend_back = (
        lax.all_gather(attend_gain, ("dp", "seq"), axis=0, tiled=True),
        lax.all_gather(attend_shift, ("dp", "seq"), axis=0, tiled=True),
        lax.all_gather(project_in, ("dp", "seq"), axis=0, tiled=True),
        lax.all_gather(project_bias, ("dp", "seq"), axis=0, tiled=True),
        lax.all_gather(project_out, ("dp", "seq"), axis=0, tiled=True),
        lax.all_gather(output_bias, ("dp", "seq"), axis=0, tiled=True),
    )
    branch_low = hidden_grad.astype(jnp.bfloat16)
    project_out_gradient = inner_rows(mixture_low, branch_low)
    output_bias_gradient = jnp.sum(branch_low.astype(jnp.float32), axis=0)
    mixture_grad = against_rows(branch_low, attend_back[4]).astype(jnp.bfloat16)

    def attend_backward(bundle):
        query_row, pairs_row, seg_query, seg_key, log_row, grad_row = bundle
        query_grad, key_grad, value_grad = backward_heads(
            split_heads(query_row),
            split_heads(pairs_row[:, :width]),
            split_heads(pairs_row[:, width:]),
            visible(seg_query, seg_key, query_place, key_place),
            log_row,
            split_heads(grad_row),
            score_scale,
        )
        pair_grad = jnp.concatenate(
            [key_grad.reshape(length, width), value_grad.reshape(length, width)], axis=1
        )
        return (query_grad.reshape(places_here, width), pair_grad)

    query_grads, pair_grads = lax.map(
        attend_backward,
        (
            query_rows,
            keys_all,
            segments,
            segments_all,
            log_totals,
            mixture_grad.reshape(rows_here, places_here, width),
        ),
    )
    pair_sums = lax.psum_scatter(
        pair_grads.astype(jnp.bfloat16), "seq", scatter_dimension=1, tiled=True
    ).astype(jnp.float32)
    projected_grad = jnp.concatenate(
        [
            query_grads.reshape(tokens_here, width).astype(jnp.bfloat16),
            pair_sums.reshape(tokens_here, 2 * width).astype(jnp.bfloat16),
        ],
        axis=1,
    )
    project_in_gradient = inner_rows(first_low, projected_grad)
    bias_sums = jnp.sum(projected_grad.astype(jnp.float32), axis=0)
    project_bias_gradient = jnp.concatenate([bias_sums[:width], bias_sums[2 * width :]])
    first_grad = against_rows(projected_grad, attend_back[2])
    attend_gain_gradient = jnp.sum(first_grad * first_normal, axis=0)
    attend_shift_gradient = jnp.sum(first_grad, axis=0)
    inputs_gradient = hidden_grad + normalize_back(
        first_grad, first_normal, first_inverse, attend_back[0].astype(jnp.float32)
    )
    attend_sums = (
        lax.psum_scatter(attend_gain_gradient, ("dp", "seq"), scatter_dimension=0, tiled=True),
        lax.psum_scatter(attend_shift_gradient, ("dp", "seq"), scatter_dimension=0, tiled=True),
        lax.psum_scatter(project_in_gradient, ("dp", "seq"), scatter_dimension=0, tiled=True),
        lax.psum_scatter(project_bias_gradient, ("dp", "seq"), scatter_dimension=0, tiled=True),
        lax.psum_scatter(project_out_gradient, ("dp", "seq"), scatter_dimension=0, tiled=True),
        lax.psum_scatter(output_bias_gradient, ("dp", "seq"), scatter_dimension=0, tiled=True),
    )
    return (
        result.astype(jnp.bfloat16).reshape(rows_here, places_here, width),
        rewards.reshape(rows_here, places_here),
        inputs_gradient.reshape(rows_here, places_here, width),
        attend_sums[0],
        attend_sums[1],
        attend_sums[2],
        attend_sums[3],
        attend_sums[4],
        attend_sums[5],
        dense_sums[0],
        dense_sums[1],
        dense_sums[2],
        dense_sums[3],
        dense_sums[4],
        dense_sums[5],
        dense_sums[6],
    )


def body(
    inputs,
    cotangent,
    segments,
    labels,
    step_ends,
    attend_gain,
    attend_shift,
    project_in,
    project_bias,
    project_out,
    output_bias,
    dense_gain,
    dense_shift,
    up_weight,
    up_bias,
    down_weight,
    down_bias,
    reward_weight,
):
    arguments = (
        inputs,
        cotangent,
        segments,
        labels,
        step_ends,
        attend_gain,
        attend_shift,
        project_in,
        project_bias,
        project_out,
        output_bias,
        dense_gain,
        dense_shift,
        up_weight,
        up_bias,
        down_weight,
        down_bias,
        reward_weight,
    )
    outcome = spread_path(arguments)
    return outcome


def solution(mesh):
    in_specs = (
        P("dp", "seq", None),
        P("dp", "seq", None),
        P("dp", "seq"),
        P("dp", "seq"),
        P("dp", "seq"),
        P(("dp", "seq")),
        P(("dp", "seq")),
        P(("dp", "seq"), None),
        P(("dp", "seq")),
        P(("dp", "seq"), None),
        P(("dp", "seq")),
        P(("dp", "seq")),
        P(("dp", "seq")),
        P(("dp", "seq"), None),
        P(("dp", "seq")),
        P(("dp", "seq"), None),
        P(("dp", "seq")),
        P(("dp", "seq")),
    )
    out_specs = (
        P("dp", "seq", None),
        P("dp", "seq"),
        P("dp", "seq", None),
        P(("dp", "seq")),
        P(("dp", "seq")),
        P(("dp", "seq"), None),
        P(("dp", "seq")),
        P(("dp", "seq"), None),
        P(("dp", "seq")),
        P(("dp", "seq")),
        P(("dp", "seq")),
        P(("dp", "seq"), None),
        P(("dp", "seq")),
        P(("dp", "seq"), None),
        P(("dp", "seq")),
        P(("dp", "seq")),
    )
    return jax.shard_map(body, mesh=mesh, in_specs=in_specs, out_specs=out_specs, check_vma=False)
```

profile of v0, /device:TPU:0, one launch (start us, length us, event | category | flops | bytes accessed | tf_op | source)
XLA Modules:
  0.0 4710.6 jit_solution(17916279258935411938)
XLA Ops:
  8.0 0.9 dynamic-update-slice.3
  8.8 0.8 dynamic-update-slice.4
  9.7 0.8 dynamic-update-slice.5
  10.5 0.8 dynamic-update-slice.2
  13.9 43.5 all-reduce.17
  57.4 66.3 %all-gather.1 = bf16[32,1,128]{2,1,0:T(2,128)(2,1)S(1)} all-gather(bf16[1,1,128]{2,1,0:T(2,128)(2,1)} %bitcast.148), channel_id=1, replica_groups=mesh['dp'=8,'seq'=4] {'dp','seq'}, dimensions={0}, use_global_device_ids=true | all-gather | bytes 8448 | tf_op jit(solution)/shard_map/all_gather | solution.py:119
  123.8 1.2 convert_reduce_fusion.2
  125.0 1.3 fusion.43
  126.3 43.7 all-gather.9.cloned.1.call-done
  170.0 11.9 fusion
  182.0 1.0 slice.44
  185.1 66.9 %all-gather.2 = bf16[32,1,256]{2,1,0:T(2,128)(2,1)S(1)} all-gather(bf16[1,1,256]{2,1,0:T(2,128)(2,1)S(1)} %reshape.327), channel_id=1, replica_groups=mesh['dp'=8,'seq'=4] {'dp','seq'}, dimensions={0}, use_global_device_ids=true | all-gather | bytes 16896 | tf_op jit(solution)/shard_map/all_gather | solution.py:168
  252.0 7.6 all_gather.58
  260.1 2.3 all-gather.17.cloned.1.call-done
  262.4 4.8 slice_bitcast_fusion
  267.2 2.9 copy.54
  270.1 1.0 fusion.67
  271.1 1.2 fusion.8
  273.4 2.2 fusion.26
  275.6 65.9 %all-gather.11.cloned.1.call-done = bf16[2048,2048]{1,0:T(8,128)(2,1)} async-done(((bf16[64,2048]{1,0:T(8,128)(2,1)}), bf16[2048,2048]{1,0:T(8,128)(2,1)}) %all-gather.11.cloned.1.call-update) | async-done | bytes 8388624 | tf_op jit(solution)/shard_map/all_gather | solution.py:120
  341.5 4.7 fusion.68
  346.5 191.2 %all-gather.13.cloned.1.call-done = bf16[2048,8192]{1,0:T(8,128)(2,1)} async-done(((bf16[64,8192]{1,0:T(8,128)(2,1)}), bf16[2048,8192]{1,0:T(8,128)(2,1)}) %all-gather.13.cloned.1.call-update) | async-done | bytes 33554448 | tf_op jit(solution)/shard_map/all_gather | solution.py:167
  537.7 17.9 convolution_add_fusion
  555.6 177.8 %all-gather.15.cloned.1.call-done = bf16[8192,2048]{1,0:T(8,128)(2,1)} async-done(((bf16[256,2048]{1,0:T(8,128)(2,1)}), bf16[8192,2048]{1,0:T(8,128)(2,1)}) %all-gather.15.cloned.1.call-update) | async-done | bytes 33554448 | tf_op jit(solution)/shard_map/all_gather | solution.py:169
  733.5 18.0 multiply_reduce_fusion.4
  751.4 19.7 convert_reduce_fusion
  771.2 19.7 multiply_reduce_fusion.2
  790.9 4.3 multiply_reduce_fusion.1
  795.1 7.1 convolution_convert_fusion
  802.2 2.0 copy.55
  804.2 3.3 fusion.19
  808.6 1.5 multiply_reduce_fusion
  810.1 1.2 multiply_convert_fusion.1
  811.2 1.3 copy-done.3
  813.3 2.2 pad_maximum_fusion
  815.5 18.8 copy.50
  834.3 10.1 copy.70
  844.4 2.9 fusion.25
  847.4 72.1 %reduce-scatter.16.cloned.1.call-done = bf16[128,4096]{1,0:T(8,128)(2,1)} async-done(((bf16[512,4096]{1,0:T(8,128)(2,1)}), bf16[128,4096]{1,0:T(8,128)(2,1)}) %reduce-scatter.16.cloned.1.call-update) | async-done | bytes 1048592
  919.4 4.6 reshape_bitcast_fusion
  924.1 5.4 copy.51
  929.4 1.7 convert_reduce_fusion.1
  931.8 14.9 fusion.42
  947.0 9.1 fusion.53
  956.2 21.0 fusion.45
  977.2 1.0 copy-done.10
  978.2 25.4 fusion.58
  1004.3 24.8 fusion.64
  1029.2 1.2 copy-done.11
  1030.4 1.4 fusion.41
  1031.8 40.8 all-reduce.20.cloned.1.call-done
  1072.5 1.3 dynamic-slice.2
  1073.8 1.3 dynamic-slice.3
  1075.1 1.3 dynamic-slice.5
  1076.3 1.3 dynamic-slice.6
  1077.6 1.3 dynamic-slice.7
  1078.8 1.3 dynamic-slice.9
  1080.1 1.3 dynamic-slice.10
  1081.4 1.3 dynamic-slice.4
  1082.6 1.3 dynamic-slice.8
  1083.9 356.7 %reduce-scatter.10.cloned.1.call-done = f32[64,2048]{1,0:T(8,128)} async-done(((f32[2048,2048]{1,0:T(8,128)}), f32[64,2048]{1,0:T(8,128)}) %reduce-scatter.10.cloned.1.call-update) | async-done | bytes 524304 | tf_op jit(solution)/shard_map/reduce_scatter | solution.py:288
  1440.6 437.0 %reduce-scatter.8.cloned.1.call-done = f32[64,6144]{1,0:T(8,128)} async-done(((f32[2048,6144]{1,0:T(8,128)}), f32[64,6144]{1,0:T(8,128)}) %reduce-scatter.8.cloned.1.call-update) | async-done | bytes 1572880 | tf_op jit(solution)/shard_map/reduce_scatter | solution.py:286
  1877.7 1412.4 %reduce-scatter.14.cloned.1.call-done = f32[256,2048]{1,0:T(8,128)} async-done(((f32[8192,2048]{1,0:T(8,128)}), f32[256,2048]{1,0:T(8,128)}) %reduce-scatter.14.cloned.1.call-update) | async-done | bytes 2097168 | tf_op jit(solution)/shard_map/reduce_scatter | solution.py:220
  3290.1 1413.6 %reduce-scatter.12.cloned.1.call-done = f32[64,8192]{1,0:T(8,128)} async-done(((f32[2048,8192]{1,0:T(8,128)}), f32[64,8192]{1,0:T(8,128)}) %reduce-scatter.12.cloned.1.call-update) | async-done | bytes 2097168 | tf_op jit(solution)/shard_map/reduce_scatter | solution.py:218
  (97 shorter events, 10.6 us)
Async XLA Ops:
  7.2 162.9 %all-gather.9.cloned.1.call-start = ((), (), s32[]{:S(2)}) async-start(), calls=%async_computation.5 | async-start | bytes 25952256 | tf_op jit(solution)/shard_map/all_gather | solution.py:118
  7.9 254.5 %all-gather.17.cloned.1.call-start = ((), (), s32[]{:S(2)}) async-start(), calls=%async_computation.13 | async-start | bytes 5242880 | tf_op jit(solution)/shard_map/all_gather | solution.py:138
  181.9 3.0 copy-start.18
  181.9 70.0 %copy-start.14 = (s32[1,128]{1,0:T(1,128)S(1)}, s32[1,128]{1,0:T(1,128)}, u32[]{:S(2)}) copy-start(s32[1,128]{1,0:T(1,128)} %param.20) | copy-start | bytes 1540
  183.0 158.4 %all-gather.11.cloned.1.call-start = ((), (), s32[]{:S(2)}) async-start(), calls=%async_computation.6 | async-start | bytes 8650752 | tf_op jit(solution)/shard_map/all_gather | solution.py:120
  183.8 353.9 %all-gather.13.cloned.1.call-start = ((), (), s32[]{:S(2)}) async-start(), calls=%async_computation.7 | async-start | bytes 34603008 | tf_op jit(solution)/shard_map/all_gather | solution.py:167
  184.3 549.1 %all-gather.15.cloned.1.call-start = ((), (), s32[]{:S(2)}) async-start(), calls=%async_computation.8 | async-start | bytes 34603008 | tf_op jit(solution)/shard_map/all_gather | solution.py:169
  184.9 734.5 %reduce-scatter.16.cloned.1.call-start = ((), (), s32[]{:S(2)}) async-start(), calls=%async_computation.14 | async-start | bytes 5242880
  185.0 352.7 %copy-start.12 = (f32[2048]{0:T(1024)}, f32[2048]{0:T(1024)S(1)}, u32[]{:S(2)}) copy-start(f32[2048]{0:T(1024)S(1)} %convert_element_type.153) | copy-start | bytes 24580
  270.1 2.3 copy-start.4
  270.1 3.3 copy-start.5
  271.1 2.0 copy-start
  273.4 68.1 %copy-start.2 = (bf16[1,128,2048]{2,1,0:T(8,128)(2,1)S(1)}, bf16[1,128,2048]{2,1,0:T(8,128)(2,1)}, u32[]{:S(2)}) copy-start(bf16[1,128,2048]{2,1,0:T(8,128)(2,1)} %param.18) | copy-start | bytes 1572868
  275.6 70.6 %copy-start.8 = (bf16[16,128,128]{2,1,0:T(8,128)(2,1)}, bf16[16,128,128]{2,1,0:T(8,128)(2,1)S(1)}, u32[]{:S(2)}) copy-start(bf16[16,128,128]{2,1,0:T(8,128)(2,1)S(1)} %fusion.26) | copy-start | bytes 1572868
  555.6 195.8 %copy-start.15 = (s32[1,128]{1,0:T(1,128)S(1)}, s32[1,128]{1,0:T(1,128)}, u32[]{:S(2)}) copy-start(s32[1,128]{1,0:T(1,128)} %param.21) | copy-start | bytes 1540
  555.6 195.8 %copy-start.16 = (s32[1,128]{1,0:T(1,128)S(1)}, s32[1,128]{1,0:T(1,128)}, u32[]{:S(2)}) copy-start(s32[1,128]{1,0:T(1,128)} %param.22) | copy-start | bytes 1540
  555.6 195.8 %copy-start.9 = (bf16[1,128,2048]{2,1,0:T(8,128)(2,1)S(1)}, bf16[1,128,2048]{2,1,0:T(8,128)(2,1)}, u32[]{:S(2)}) copy-start(bf16[1,128,2048]{2,1,0:T(8,128)(2,1)} %param.19) | copy-start | bytes 1572868
  751.4 19.8 copy-start.17
  804.2 3.6 copy-start.1
  804.2 4.3 copy-start.6
  804.2 4.3 copy-start.7
  811.2 1.3 copy-start.3
  844.4 228.2 %all-reduce.20.cloned.1.call-start = ((), (), s32[]{:S(2)}) async-start(), calls=%async_computation.15 | async-start | bytes 212992
  946.7 493.9 %reduce-scatter.10.cloned.1.call-start = ((), (), s32[]{:S(2)}) async-start(), calls=%async_computation.10 | async-start | bytes 17301504 | tf_op jit(solution)/shard_map/reduce_scatter | solution.py:288
  956.1 921.5 %reduce-scatter.8.cloned.1.call-start = ((), (), s32[]{:S(2)}) async-start(), calls=%async_computation.9 | async-start | bytes 51904512 | tf_op jit(solution)/shard_map/reduce_scatter | solution.py:286
  977.2 1.0 copy-start.10
  977.2 2312.9 %reduce-scatter.14.cloned.1.call-start = ((), (), s32[]{:S(2)}) async-start(), calls=%async_computation.12 | async-start | bytes 69206016 | tf_op jit(solution)/shard_map/reduce_scatter | solution.py:220
  1003.6 0.7 copy-start.13
  1003.6 3700.0 %reduce-scatter.12.cloned.1.call-start = ((), (), s32[]{:S(2)}) async-start(), calls=%async_computation.11 | async-start | bytes 69206016 | tf_op jit(solution)/shard_map/reduce_scatter | solution.py:218
  1029.1 1.2 copy-start.11
Sparse Core Ops, SparseCore 0:
  10.9 159.0 all-gather.8
  183.1 79.2 all-gather.16
  265.4 76.0 all-gather.10
  344.3 193.3 all-gather.12
  540.5 192.9 all-gather.14
  844.5 74.9 reduce-scatter.15
  946.9 125.6 all-reduce.19
  1075.4 365.1 reduce-scatter.9
  1447.6 429.9 reduce-scatter.7
  1880.4 1409.5 reduce-scatter.13
  3293.0 1410.5 reduce-scatter.11
where the time goes:
time: 4720 us; the launch traced here: 4710 us
  waiting for transfers between devices  4220 us (89%)
  matrix products  206 us (4%)
  blocking collectives  184 us (4%)
  local copies, waits for them, and re-layouts  73.4 us (2%)
    reduce_scatter x1, waiting for transfers between devices, spread_path(): lax.psum_scatter(up_weight_gradient, ('dp', 'seq'), scatter_dimension=0,...  1410 us
    reduce_scatter x1, waiting for transfers between devices, spread_path(): lax.psum_scatter(down_weight_gradient, ('dp', 'seq'), scatter_dimension=0...  1410 us
    reduce_scatter x1, waiting for transfers between devices, spread_path(): lax.psum_scatter(project_in_gradient, ('dp', 'seq'), scatter_dimension=0,...  437 us
    reduce_scatter x1, waiting for transfers between devices, spread_path(): lax.psum_scatter(project_out_gradient, ('dp', 'seq'), scatter_dimension=0...  357 us
    all_gather x1, waiting for transfers between devices, spread_path(): lax.all_gather(up_weight, ('dp', 'seq'), axis=0, tiled=True)  191 us
    all_gather x1, waiting for transfers between devices, spread_path(): lax.all_gather(down_weight, ('dp', 'seq'), axis=0, tiled=True)  178 us
    unnamed x13, waiting for transfers between devices  115 us
  transfers between devices with their start and end apart: 11, of which 11 were waited for; matrix products, arithmetic and copies ran while one was open for 3% of the time, Pallas kernels for 0%

commit v1 on v0

v1 whole, which is shorter than its diff:
```python
from functools import partial

import jax
import jax.numpy as jnp
from jax import lax
from jax.sharding import PartitionSpec as P

HEADS = 16
EPSILON = 1e-05
MASKED = -1e30
LOW = jnp.bfloat16
WIDE = jnp.float32
EVERY = ("dp", "seq")


def product(left, right):
    return jnp.dot(left, right, preferred_element_type=WIDE)


def inner_rows(left, right):
    return jnp.einsum("ta,tb->ab", left, right, preferred_element_type=WIDE)


def against_rows(left, right):
    return jnp.einsum("tb,ab->ta", left, right, preferred_element_type=WIDE)


def normalize_parts(field, gain, shift):
    center = field - jnp.mean(field, axis=-1, keepdims=True)
    spread = jnp.mean(center * center, axis=-1, keepdims=True)
    inverse = lax.rsqrt(spread + EPSILON)
    normal = center * inverse
    return (normal * gain + shift, normal, inverse)


def normalize_back(upstream, normal, inverse, gain):
    scaled = upstream * gain
    mean_scaled = jnp.mean(scaled, axis=-1, keepdims=True)
    mean_cross = jnp.mean(scaled * normal, axis=-1, keepdims=True)
    return inverse * (scaled - mean_scaled - normal * mean_cross)


def ring_next():
    size = lax.axis_size("seq")
    return [(place, (place + 1) % size) for place in range(size)]


def ring_gather(block):
    blocks = [block]
    for _ in range(lax.axis_size("seq") - 1):
        block = lax.ppermute(block, "seq", ring_next())
        blocks.append(block)
    return blocks


def ring_sum(parts):
    total = parts[1]
    for part in parts[2:] + parts[:1]:
        total = lax.ppermute(total.astype(LOW), "seq", ring_next()).astype(WIDE) + part
    return total


def to_ring(table):
    size = lax.axis_size("seq")
    me = lax.axis_index("seq")
    return jnp.stack(
        [lax.dynamic_index_in_dim(table, (me - k) % size, 0, keepdims=False) for k in range(size)]
    )


def head_split():
    groups, ranks = lax.axis_size("dp"), lax.axis_size("seq")
    blocks = groups * ranks // HEADS
    if blocks <= ranks:
        return ((blocks, groups // blocks, ranks // blocks), (2, 0, 1))
    return ((HEADS // ranks, ranks), (1, 0))


def heads_by_rank(table):
    split, order = head_split()
    width = table.shape[-1]
    moved = table.reshape(split + (width,)).transpose(order + (len(split),))
    return moved.reshape(lax.axis_size("seq"), -1)


def heads_from_rank(table):
    split, order = head_split()
    width = table.size // HEADS
    back = [order.index(axis) for axis in range(len(order))]
    moved = table.reshape(tuple(split[axis] for axis in order) + (width,))
    return moved.transpose(tuple(back) + (len(split),)).reshape(HEADS, width)


def out_route():
    groups, ranks = lax.axis_size("dp"), lax.axis_size("seq")
    blocks = groups * ranks // HEADS
    route = []
    for group in range(groups):
        for rank in range(ranks):
            if blocks <= ranks:
                held = groups // blocks
                high, low = divmod(group, held)
                pair, part = divmod(rank, blocks)
                target = (part * held + low, pair * blocks + high)
            else:
                span = blocks // ranks
                head, extra = divmod(group, span)
                high, low = divmod(head, ranks)
                target = ((high * ranks + rank) * span + extra, low)
            route.append((group * ranks + rank, target[0] * ranks + target[1]))
    return route


def out_parts():
    groups, ranks = lax.axis_size("dp"), lax.axis_size("seq")
    blocks = groups * ranks // HEADS
    if blocks <= ranks:
        return ((blocks, groups // blocks), (1, 0))
    return ((HEADS // ranks, ranks, blocks // ranks), (0, 2, 1))


def out_gather(block):
    moved = lax.ppermute(block, EVERY, out_route())
    whole = lax.all_gather(moved, "dp", axis=0, tiled=False)
    split, order = out_parts()
    tail = tuple(range(len(split), len(split) + 2))
    return whole.reshape(split + block.shape).transpose(order + tail).reshape(-1, block.shape[1])


def out_scatter(gradient, rows):
    split, order = out_parts()
    back = tuple(order.index(axis) for axis in range(len(order)))
    tail = tuple(range(len(split), len(split) + 2))
    width = gradient.shape[1]
    parted = gradient.reshape(tuple(split[axis] for axis in order) + (rows, width))
    parted = parted.transpose(back + tail).reshape(-1, width)
    summed = scatter_groups(parted)
    return lax.ppermute(summed, EVERY, [(there, here) for here, there in out_route()])


def gather_groups(block):
    return lax.all_gather(block, "dp", axis=0, tiled=True)


def scatter_groups(gradient):
    return lax.psum_scatter(gradient.astype(LOW), "dp", scatter_dimension=0, tiled=True)


def swap_ranks(blocks):
    return lax.all_to_all(blocks, "seq", split_axis=0, concat_axis=0, tiled=True)


def spread_path(
    inputs,
    cotangent,
    segments,
    labels,
    step_ends,
    attend_gain,
    attend_shift,
    project_in,
    project_bias,
    project_out,
    output_bias,
    dense_gain,
    dense_shift,
    up_weight,
    up_bias,
    down_weight,
    down_bias,
    reward_weight,
):
    groups, ranks = lax.axis_size("dp"), lax.axis_size("seq")
    rank = lax.axis_index("seq")
    rows_here, places_here, width = inputs.shape
    all_rows = rows_here * groups
    head_width = width // HEADS
    heads_here = HEADS // ranks
    share = heads_here * head_width
    rows_in = project_in.shape[0]
    hidden_here = down_weight.shape[0]
    length = ranks * places_here
    score_scale = head_width ** (-0.5)

    small = (
        attend_gain,
        attend_shift,
        project_bias,
        output_bias,
        dense_gain,
        dense_shift,
        up_bias,
        down_bias,
        reward_weight,
    )
    sizes = [vector.shape[0] for vector in small]
    gathered = lax.all_gather(jnp.concatenate(small), EVERY, axis=0, tiled=False).astype(WIDE)
    vectors = []
    start = 0
    for size in sizes:
        vectors.append(gathered[:, start : start + size].reshape(-1))
        start += size
    gain_one, shift_one, bias_in, bias_out, gain_two, shift_two, bias_up, bias_down, reward_wide = (
        vectors
    )

    def own_heads(vector):
        return lax.dynamic_index_in_dim(
            heads_by_rank(vector.reshape(HEADS, head_width)), rank, 0, keepdims=False
        )

    bias_full = jnp.concatenate(
        [own_heads(bias_in[:width]), jnp.zeros((share,), WIDE), own_heads(bias_in[width:])]
    )
    bias_up_here = lax.dynamic_index_in_dim(
        bias_up.reshape(groups, ranks, hidden_here), rank, 1, keepdims=False
    ).reshape(-1)
    marks = lax.all_gather(
        jnp.stack([segments[0], labels[0], step_ends[0]]), "seq", axis=0, tiled=False
    )
    marks_ring = to_ring(marks)
    segments_ring = marks_ring[:, 0].reshape(-1)
    places_ring = to_ring(jnp.arange(length).reshape(ranks, places_here)).reshape(-1)

    pieces = project_in.reshape(rows_in, 3, HEADS, head_width)
    columns_in = jnp.stack(
        [
            jnp.concatenate([part[rank_] for part in parts], axis=1)
            for parts in [
                [
                    heads_by_rank(
                        pieces[:, which].transpose(1, 0, 2).reshape(HEADS, rows_in * head_width)
                    )
                    .reshape(ranks, heads_here, rows_in, head_width)
                    .transpose(0, 2, 1, 3)
                    .reshape(ranks, rows_in, share)
                    for which in range(3)
                ]
            ]
            for rank_ in range(ranks)
        ]
    )
    weight_in = gather_groups(swap_ranks(columns_in).reshape(ranks * rows_in, 3 * share))
    weight_out = out_gather(project_out)
    columns_up = up_weight.reshape(rows_in, groups, ranks, hidden_here).transpose(2, 0, 1, 3)
    columns_up = columns_up.reshape(ranks, rows_in, groups * hidden_here)
    weight_up = gather_groups(swap_ranks(columns_up).reshape(ranks * rows_in, groups * hidden_here))
    weight_down = gather_groups(down_weight)

    inputs_ring = ring_gather(inputs[0])
    own = inputs[0].astype(WIDE)
    firsts = []
    shifted = []
    for block in inputs_ring:
        value, normal, inverse = normalize_parts(block.astype(WIDE), gain_one, shift_one)
        if not firsts:
            first_normal, first_inverse = normal, inverse
        firsts.append(value.astype(LOW))
        shifted.append((product(firsts[-1], weight_in) + bias_full).astype(LOW))
    first_low = jnp.concatenate(firsts)
    projected = jnp.concatenate(shifted)

    def heads(block):
        return block.reshape(length, heads_here, head_width)

    queries, keys, values = (
        heads(projected[:, :share]),
        heads(projected[:, share : 2 * share]),
        heads(projected[:, 2 * share :]),
    )
    same = (segments_ring[None, :] == 0) | (segments_ring[None, :] == segments_ring[:, None])
    allowed = same & (places_ring[None, :] <= places_ring[:, None])
    scores = jnp.einsum("qhd,khd->hqk", queries, keys, preferred_element_type=WIDE) * score_scale
    scores = jnp.where(allowed[None], scores, MASKED)
    highest = jnp.max(scores, axis=-1, keepdims=True)
    exponent = jnp.exp(scores - highest)
    totals = jnp.sum(exponent, axis=-1, keepdims=True)
    chances = exponent / totals
    chances_low = chances.astype(LOW)
    mixture = jnp.einsum("hqk,khd->qhd", chances_low, values, preferred_element_type=WIDE)
    mixture = mixture.reshape(length, share).astype(LOW)

    def block_of(array, k):
        return array[k * places_here : (k + 1) * places_here]

    branch = ring_sum([product(block_of(mixture, k), weight_out) for k in range(ranks)])
    hidden = own + branch + bias_out

    second_value, second_normal, second_inverse = normalize_parts(hidden, gain_two, shift_two)
    seconds = ring_gather(second_value.astype(LOW))
    upwards = [product(block, weight_up) + bias_up_here for block in seconds]
    activated = [jax.nn.gelu(block, approximate=True).astype(LOW) for block in upwards]
    dense_parts = [product(block, weight_down) for block in activated]

    reward_parts = [jnp.sum(part * reward_wide, axis=-1) for part in dense_parts]
    reward_parts[0] = reward_parts[0] + jnp.sum((hidden + bias_down) * reward_wide, axis=-1)
    rewards_all = lax.psum(to_ring(jnp.stack(reward_parts)), "seq")
    scored = (marks[:, 2] * (marks[:, 0] > 0)).astype(WIDE)
    error_all = scored * (jax.nn.sigmoid(rewards_all) - marks[:, 1].astype(WIDE)) / all_rows
    error_ring = to_ring(error_all)
    rewards = lax.dynamic_index_in_dim(rewards_all, rank, 0, keepdims=False)
    cotangents = ring_gather(cotangent[0])
    result_grads = [
        block.astype(WIDE) + error_ring[k][:, None] * reward_wide
        for k, block in enumerate(cotangents)
    ]
    dense_lows = [block.astype(LOW) for block in result_grads]
    result_grad = result_grads[0]
    result = hidden + ring_sum(dense_parts) + bias_down
    reward_weight_gradient = jnp.sum(error_ring[0][:, None] * result, axis=0)
    down_bias_gradient = jnp.sum(dense_lows[0].astype(WIDE), axis=0)

    upward_lows = []
    for k in range(ranks):
        _, pull = jax.vjp(partial(jax.nn.gelu, approximate=True), upwards[k])
        upward_lows.append(pull(against_rows(dense_lows[k], weight_down))[0].astype(LOW))
    second_grad = ring_sum([against_rows(block, weight_up) for block in upward_lows])
    activated_all = jnp.concatenate(activated)
    upward_all = jnp.concatenate(upward_lows)
    down_weight_gradient = scatter_groups(inner_rows(activated_all, jnp.concatenate(dense_lows)))
    up_weight_gradient = scatter_groups(inner_rows(jnp.concatenate(seconds), upward_all))
    up_weight_gradient = swap_ranks(
        up_weight_gradient.reshape(ranks, rows_in, groups * hidden_here)
    )
    up_weight_gradient = (
        up_weight_gradient.reshape(ranks, rows_in, groups, hidden_here)
        .transpose(1, 2, 0, 3)
        .reshape(up_weight.shape)
    )
    up_bias_gradient = jnp.sum(upward_all.astype(WIDE), axis=0)
    dense_gain_gradient = jnp.sum(second_grad * second_normal, axis=0)
    dense_shift_gradient = jnp.sum(second_grad, axis=0)
    hidden_grad = result_grad + normalize_back(second_grad, second_normal, second_inverse, gain_two)

    branch_low = hidden_grad.astype(LOW)
    branch_lows = ring_gather(branch_low)
    output_bias_gradient = jnp.sum(branch_low.astype(WIDE), axis=0)
    mixture_grad = jnp.concatenate([against_rows(block, weight_out) for block in branch_lows])
    mixture_grad = mixture_grad.astype(LOW)
    project_out_gradient = out_scatter(
        inner_rows(mixture, jnp.concatenate(branch_lows)), project_out.shape[0]
    )
    grad_heads = heads(mixture_grad)
    chance_grad = jnp.einsum("qhd,khd->hqk", grad_heads, values, preferred_element_type=WIDE)
    weighted = jnp.sum(chances * chance_grad, axis=-1, keepdims=True)
    score_grad = (chances * (chance_grad - weighted)).astype(LOW)
    query_grad = jnp.einsum("hqk,khd->qhd", score_grad, keys, preferred_element_type=WIDE)
    key_grad = jnp.einsum("hqk,qhd->khd", score_grad, queries, preferred_element_type=WIDE)
    value_grad = jnp.einsum("hqk,qhd->khd", chances_low, grad_heads, preferred_element_type=WIDE)
    projected_grad = jnp.concatenate(
        [
            (query_grad * score_scale).reshape(length, share).astype(LOW),
            (key_grad * score_scale).reshape(length, share).astype(LOW),
            value_grad.reshape(length, share).astype(LOW),
        ],
        axis=1,
    )
    first_grad = ring_sum(
        [against_rows(block_of(projected_grad, k), weight_in) for k in range(ranks)]
    )
    project_in_gradient = scatter_groups(inner_rows(first_low, projected_grad))
    project_in_gradient = swap_ranks(project_in_gradient.reshape(ranks, rows_in, 3 * share))
    project_in_gradient = project_in_gradient.reshape(ranks, rows_in, 3, heads_here, head_width)
    project_in_gradient = jnp.concatenate(
        [
            heads_from_rank(
                project_in_gradient[:, :, which].transpose(0, 2, 1, 3).reshape(ranks, -1)
            )
            .reshape(HEADS, rows_in, head_width)
            .transpose(1, 0, 2)
            .reshape(rows_in, width)
            for which in range(3)
        ],
        axis=1,
    )
    bias_sums = jnp.sum(projected_grad.astype(WIDE), axis=0)

    def place_heads(vector):
        table = jnp.zeros((ranks, share), WIDE)
        return heads_from_rank(
            lax.dynamic_update_index_in_dim(table, vector, rank, 0)
        ).reshape(-1)

    project_bias_gradient = jnp.concatenate(
        [place_heads(bias_sums[:share]), place_heads(bias_sums[2 * share :])]
    )
    up_bias_gradient = lax.dynamic_update_index_in_dim(
        jnp.zeros((groups, ranks, hidden_here), WIDE),
        up_bias_gradient.reshape(groups, hidden_here),
        rank,
        1,
    ).reshape(-1)
    attend_gain_gradient = jnp.sum(first_grad * first_normal, axis=0)
    attend_shift_gradient = jnp.sum(first_grad, axis=0)
    inputs_gradient = hidden_grad + normalize_back(
        first_grad, first_normal, first_inverse, gain_one
    )
    sums = (
        attend_gain_gradient,
        attend_shift_gradient,
        project_bias_gradient,
        output_bias_gradient,
        dense_gain_gradient,
        dense_shift_gradient,
        up_bias_gradient,
        down_bias_gradient,
        reward_weight_gradient,
    )
    table = jnp.concatenate([vector.reshape(groups * ranks, -1) for vector in sums], axis=1)
    summed = lax.psum_scatter(table, EVERY, scatter_dimension=0, tiled=True)[0]
    parts = []
    start = 0
    for size in sizes:
        parts.append(summed[start : start + size])
        start += size
    return (
        result.astype(LOW)[None],
        rewards[None],
        inputs_gradient[None],
        parts[0],
        parts[1],
        project_in_gradient.astype(WIDE),
        parts[2],
        project_out_gradient.astype(WIDE),
        parts[3],
        parts[4],
        parts[5],
        up_weight_gradient.astype(WIDE),
        parts[6],
        down_weight_gradient.astype(WIDE),
        parts[7],
        parts[8],
    )


def solution(mesh):
    row = P("dp", "seq")
    wide_row = P("dp", "seq", None)
    vector = P(("dp", "seq"))
    matrix = P(("dp", "seq"), None)
    in_specs = (
        wide_row,
        wide_row,
        row,
        row,
        row,
        vector,
        vector,
        matrix,
        vector,
        matrix,
        vector,
        vector,
        vector,
        matrix,
        vector,
        matrix,
        vector,
        vector,
    )
    out_specs = (
        wide_row,
        row,
        wide_row,
        vector,
        vector,
        matrix,
        vector,
        matrix,
        vector,
        vector,
        vector,
        matrix,
        vector,
        matrix,
        vector,
        vector,
    )
    return jax.shard_map(
        spread_path, mesh=mesh, in_specs=in_specs, out_specs=out_specs, check_vma=False
    )
```

time: 4720 us -> 870 us (0.18)
  waiting for transfers between devices: 4220 us -> 519 us
  matrix products: 206 us -> 123 us
  blocking collectives: 184 us -> 124 us
    reduce_scatter x4, waiting for transfers between devices: 3620 us -> 162 us  [scatter_groups(): lax.psum_scatter(gradient.astype(LOW), 'dp', scatter_dimension=0, tiled=T...]
    all_gather x5 -> x4, waiting for transfers between devices: 481 us -> 0.04 us  [the longest x3 0.04 us: gather_groups(): return lax.all_gather(block, 'dp', axis=0, tiled=True)]
    ppermute x0 -> x26, waiting for transfers between devices: none -> 213 us  [the longest x12 107 us: ring_sum(): lax.ppermute(total.astype(LOW), 'seq', ring_next()).astype(WIDE) + part]
    all_gather x3 -> x1, blocking collectives: 141 us -> 12.4 us  [spread_path(): lax.all_gather(jnp.stack([segments[0], labels[0], step_ends[0]]), 'seq',...]
    dot_general x18 -> x41, matrix products: 206 us -> 120 us  [the longest x16 52.1 us: against_rows(): return jnp.einsum('tb,ab->ta', left, right, preferred_element_type=WIDE)]
    all_to_all x0 -> x2, blocking collectives: none -> 62.8 us  [swap_ranks(): lax.all_to_all(blocks, 'seq', split_axis=0, concat_axis=0, tiled=True)]
    unnamed x67 -> x197, local copies, waits for them, and re-layouts: 67.1 us -> 10.4 us
    unnamed x13 -> x10, waiting for transfers between devices: 115 us -> 121 us
  transfers between devices with their start and end apart: 11 -> 37, of which waited for: 11 -> 26; matrix products, arithmetic and copies ran while one was open for 3% -> 16% of each run, Pallas kernels for 0% -> 0%
where the time goes in v1:
time: 870 us; the launch traced here: 862 us
  waiting for transfers between devices  519 us (60%)
  blocking collectives  124 us (14%)
  matrix products  123 us (14%)
  local copies, waits for them, and re-layouts  34.4 us (4%)
  other arithmetic  23.6 us (3%)
  starting transfers between devices  21.7 us (2%)
  between operations  16.1 us (2%)
    reduce_scatter x4, waiting for transfers between devices, scatter_groups(): lax.psum_scatter(gradient.astype(LOW), 'dp', scatter_dimension=0, tiled=T...  162 us
    unnamed x10, waiting for transfers between devices  121 us
    ppermute x12, waiting for transfers between devices, ring_sum(): lax.ppermute(total.astype(LOW), 'seq', ring_next()).astype(WIDE) + part  107 us
    ppermute x12, waiting for transfers between devices, ring_gather(): block = lax.ppermute(block, 'seq', ring_next())  106 us
    all_to_all x2, blocking collectives, swap_ranks(): lax.all_to_all(blocks, 'seq', split_axis=0, concat_axis=0, tiled=True)  62.8 us
    dot_general x16, matrix products, against_rows(): return jnp.einsum('tb,ab->ta', left, right, preferred_element_type=WIDE)  52.1 us
    unnamed x1, blocking collectives  39.9 us
    dot_general x16, matrix products, product(): return jnp.dot(left, right, preferred_element_type=WIDE)  35.8 us
  transfers between devices with their start and end apart: 37, of which 26 were waited for; matrix products, arithmetic and copies ran while one was open for 16% of the time, Pallas kernels for 0%

profile of v1, /device:TPU:0, one launch (start us, length us, event | category | flops | bytes accessed | tf_op | source)
XLA Modules:
  0.0 862.3 jit_solution(12573582679282220542)
XLA Ops:
  14.2 34.9 %all_to_all.20 = bf16[4,64,1536]{2,1,0:T(8,128)(2,1)} all-to-all(bf16[4,64,1536]{2,1,0:T(8,128)(2,1)S(1)} %pad_maximum_fusion.3), channel_id=1, replica_groups=mesh['dp'=8,'seq'=4] {'seq'}, dimensions={0} | all-to-all | bytes 1572864 | tf_op jit(solution)/shard_map/all_to_all | solution.py:150
  50.9 27.9 %all_to_all.21 = bf16[4,64,2048]{2,1,0:T(8,128)(2,1)} all-to-all(bf16[4,64,2048]{2,1,0:T(8,128)(2,1)S(1)} %reshape.432), channel_id=1, replica_groups=mesh['dp'=8,'seq'=4] {'seq'}, dimensions={0} | all-to-all | bytes 2097152 | tf_op jit(solution)/shard_map/all_to_all | solution.py:150
  80.1 39.9 %all-reduce = bf16[26624]{0:T(1024)(128)(2,1)S(1)} all-reduce(bf16[26624]{0:T(1024)(128)(2,1)S(1)} %dynamic-update-slice), channel_id=2, replica_groups=mesh['dp'=8,'seq'=4] {'dp','seq'}, use_global_device_ids=true, to_apply=%add | all-reduce | flops 26624 | bytes 106496
  121.1 12.4 %all-gather.3 = s32[4,3,128]{2,1,0:T(4,128)S(1)} all-gather(s32[1,3,128]{2,1,0:T(4,128)S(1)} %add_bitcast_fusion), channel_id=3, replica_groups=mesh['dp'=8,'seq'=4] {'seq'}, dimensions={0}, use_global_device_ids=true | all-gather | bytes 7680 | tf_op jit(solution)/shard_map/all_gather | solution.py:218
  135.1 12.3 %collective-permute-done.1 = bf16[128,2048]{1,0:T(8,128)(2,1)S(1)} collective-permute-done((bf16[128,2048]{1,0:T(8,128)(2,1)S(1)}, bf16[128,2048]{1,0:T(8,128)(2,1)S(1)}, u32[]{:S(2)}, u32[]{:S(2)}) %collective-permute-start.1) | collective-permute-done | bytes 524320 | tf_op jit(solution)/shard_map/ppermute | solution.py:51
  148.1 11.5 %collective-permute-done.2 = bf16[128,2048]{1,0:T(8,128)(2,1)S(1)} collective-permute-done((bf16[128,2048]{1,0:T(8,128)(2,1)S(1)}, bf16[128,2048]{1,0:T(8,128)(2,1)S(1)}, u32[]{:S(2)}, u32[]{:S(2)}) %collective-permute-start.2) | collective-permute-done | bytes 524320 | tf_op jit(solution)/shard_map/ppermute | solution.py:51
  161.8 2.4 copy.190
  164.3 4.3 fusion.6
  175.3 3.8 fusion.161
  179.1 2.9 convolution_convert_fusion.8
  183.3 11.5 %collective-permute-done.4 = bf16[128,2048]{1,0:T(8,128)(2,1)S(1)} collective-permute-done((bf16[128,2048]{1,0:T(8,128)(2,1)S(1)}, bf16[128,2048]{1,0:T(8,128)(2,1)S(1)}, u32[]{:S(2)}, u32[]{:S(2)}) %collective-permute-start.4) | collective-permute-done | bytes 524320 | tf_op jit(solution)/shard_map/ppermute | solution.py:59
  195.4 12.3 %collective-permute-done.5 = bf16[128,2048]{1,0:T(8,128)(2,1)S(1)} collective-permute-done((bf16[128,2048]{1,0:T(8,128)(2,1)S(1)}, bf16[128,2048]{1,0:T(8,128)(2,1)S(1)}, u32[]{:S(2)}, u32[]{:S(2)}) %collective-permute-start.5) | collective-permute-done | bytes 524320 | tf_op jit(solution)/shard_map/ppermute | solution.py:59
  208.7 16.2 %collective-permute-done.6 = bf16[128,2048]{1,0:T(8,128)(2,1)S(1)} collective-permute-done((bf16[128,2048]{1,0:T(8,128)(2,1)S(1)}, bf16[128,2048]{1,0:T(8,128)(2,1)S(1)}, u32[]{:S(2)}, u32[]{:S(2)}) %collective-permute-start.6) | collective-permute-done | bytes 524320 | tf_op jit(solution)/shard_map/ppermute | solution.py:59
  225.7 1.8 fusion.148
  228.9 7.3 collective-permute-done.13
  236.2 11.2 %collective-permute-done.7 = bf16[128,2048]{1,0:T(8,128)(2,1)} collective-permute-done((bf16[128,2048]{1,0:T(8,128)(2,1)S(1)}, bf16[128,2048]{1,0:T(8,128)(2,1)}, u32[]{:S(2)}, u32[]{:S(2)}) %collective-permute-start.7) | collective-permute-done | bytes 524320 | tf_op jit(solution)/shard_map/ppermute | solution.py:51
  247.6 11.1 %collective-permute-done.15 = bf16[128,2048]{1,0:T(8,128)(2,1)} collective-permute-done((bf16[128,2048]{1,0:T(8,128)(2,1)}, bf16[128,2048]{1,0:T(8,128)(2,1)}, u32[]{:S(2)}, u32[]{:S(2)}) %collective-permute-start.15) | collective-permute-done | bytes 524320 | tf_op jit(solution)/shard_map/ppermute | solution.py:51
  258.7 11.2 %collective-permute-done.9 = bf16[128,2048]{1,0:T(8,128)(2,1)} collective-permute-done((bf16[128,2048]{1,0:T(8,128)(2,1)}, bf16[128,2048]{1,0:T(8,128)(2,1)}, u32[]{:S(2)}, u32[]{:S(2)}) %collective-permute-start.9) | collective-permute-done | bytes 524320 | tf_op jit(solution)/shard_map/ppermute | solution.py:51
  270.4 6.3 multiply_convert_fusion.4
  276.8 5.0 fusion.162
  282.7 2.6 multiply_convert_fusion.1
  285.3 3.9 multiply_convert_fusion.3
  290.7 3.7 multiply_convert_fusion.2
  300.2 9.8 %collective-permute-done.10 = bf16[128,2048]{1,0:T(8,128)(2,1)S(1)} collective-permute-done((bf16[128,2048]{1,0:T(8,128)(2,1)S(1)}, bf16[128,2048]{1,0:T(8,128)(2,1)S(1)}, u32[]{:S(2)}, u32[]{:S(2)}) %collective-permute-start.10) | collective-permute-done | bytes 524320 | tf_op jit(solution)/shard_map/ppermute | solution.py:59
  311.2 8.5 psum.7
  319.8 2.3 convert_reduce_fusion.6
  322.2 8.2 fusion.85
  330.4 2.9 convolution_convert_fusion.4
  333.3 2.0 collective-permute-start.14
  335.5 3.3 fusion.106
  338.8 3.3 fusion.99
  342.1 3.3 fusion.92
  345.4 1.8 collective-permute-done.14
  347.2 2.9 add_convert_fusion.4
  351.3 2.9 fusion.165
  354.2 10.6 %collective-permute-done.16 = bf16[128,2048]{1,0:T(8,128)(2,1)S(1)} collective-permute-done((bf16[128,2048]{1,0:T(8,128)(2,1)S(1)}, bf16[128,2048]{1,0:T(8,128)(2,1)S(1)}, u32[]{:S(2)}, u32[]{:S(2)}) %collective-permute-start.16) | collective-permute-done | bytes 524320 | tf_op jit(solution)/shard_map/ppermute | solution.py:59
  366.5 2.9 fusion.166
  369.4 6.9 collective-permute-done.18
  377.9 2.6 convert_reduce_fusion.7
  381.3 15.9 %collective-permute-done.19 = bf16[128,2048]{1,0:T(8,128)(2,1)S(1)} collective-permute-done((bf16[128,2048]{1,0:T(8,128)(2,1)S(1)}, bf16[128,2048]{1,0:T(8,128)(2,1)S(1)}, u32[]{:S(2)}, u32[]{:S(2)}) %collective-permute-start.19) | collective-permute-done | bytes 524320 | tf_op jit(solution)/shard_map/ppermute | solution.py:51
  398.0 14.9 %collective-permute-done.20 = bf16[128,2048]{1,0:T(8,128)(2,1)S(1)} collective-permute-done((bf16[128,2048]{1,0:T(8,128)(2,1)S(1)}, bf16[128,2048]{1,0:T(8,128)(2,1)S(1)}, u32[]{:S(2)}, u32[]{:S(2)}) %collective-permute-start.20) | collective-permute-done | bytes 524320 | tf_op jit(solution)/shard_map/ppermute | solution.py:51
  414.6 9.3 %collective-permute-done.21 = bf16[128,2048]{1,0:T(8,128)(2,1)S(1)} collective-permute-done((bf16[128,2048]{1,0:T(8,128)(2,1)S(1)}, bf16[128,2048]{1,0:T(8,128)(2,1)S(1)}, u32[]{:S(2)}, u32[]{:S(2)}) %collective-permute-start.21) | collective-permute-done | bytes 524320 | tf_op jit(solution)/shard_map/ppermute | solution.py:51
  430.4 5.4 convolution_convert_fusion.2
  436.9 2.5 fusion.2
  441.1 5.7 convolution_convert_fusion.5
  446.8 13.9 %collective-permute-done.22 = bf16[128,2048]{1,0:T(8,128)(2,1)S(1)} collective-permute-done((bf16[128,2048]{1,0:T(8,128)(2,1)S(1)}, bf16[128,2048]{1,0:T(8,128)(2,1)S(1)}, u32[]{:S(2)}, u32[]{:S(2)}) %collective-permute-start.22) | collective-permute-done | bytes 524320 | tf_op jit(solution)/shard_map/ppermute | solution.py:59
  460.7 5.2 add_convert_fusion.1
  466.0 2.2 fusion.122
  468.3 11.7 %collective-permute-done.23 = bf16[128,2048]{1,0:T(8,128)(2,1)S(1)} collective-permute-done((bf16[128,2048]{1,0:T(8,128)(2,1)S(1)}, bf16[128,2048]{1,0:T(8,128)(2,1)S(1)}, u32[]{:S(2)}, u32[]{:S(2)}) %collective-permute-start.23) | collective-permute-done | bytes 524320 | tf_op jit(solution)/shard_map/ppermute | solution.py:59
  481.9 10.3 %collective-permute-done.24 = bf16[128,2048]{1,0:T(8,128)(2,1)} collective-permute-done((bf16[128,2048]{1,0:T(8,128)(2,1)}, bf16[128,2048]{1,0:T(8,128)(2,1)}, u32[]{:S(2)}, u32[]{:S(2)}) %collective-permute-start.24) | collective-permute-done | bytes 524320 | tf_op jit(solution)/shard_map/ppermute | solution.py:59
  492.2 6.2 fusion.65
  499.5 9.6 %convolution_convert_fusion = bf16[2048,2048]{1,0:T(8,128)(2,1)} fusion(bf16[128,2048]{1,0:T(8,128)(2,1)} %copy-done.15, bf16[128,2048]{1,0:T(8,128)(2,1)S(1)} %copy-done.13, bf16[128,2048]{1,0:T(8,128)(2,1)S(1)} %copy-done.8, bf16[128,2048]{1,0:T(8,128)(2,1)} %copy-done.14, bf16[128,2048]{1,0:T(8,128)(2,1)} %copy-done.57, bf16[128,2048]{1,0:T(8,128)(2,1)} %copy-done.56, ...), kind=kOutput, calls=%fused_computation.1 | convolution fusion | flops 4315938816 | bytes 12582912 | tf_op jit(solution)/shard_map/ta,tb->ab/dot_general | solution.py:21
  510.9 8.3 convolution_convert_fusion.1
  519.9 3.6 all-to-all-start.2
  523.5 20.3 %reduce-scatter.7.cloned.1.call-done = bf16[64,2048]{1,0:T(8,128)(2,1)} async-done(((bf16[512,2048]{1,0:T(8,128)(2,1)}), bf16[64,2048]{1,0:T(8,128)(2,1)}) %reduce-scatter.7.cloned.1.call-update) | async-done | bytes 262160 | tf_op jit(solution)/shard_map/reduce_scatter | solution.py:146
  543.8 3.6 collective-permute-start.25
  547.4 2.5 fusion.64
  549.9 120.8 %all-reduce.4.cloned.1.call-done = f32[32,832]{1,0:T(8,128)} async-done(((f32[32,832]{1,0:T(8,128)}), f32[32,832]{1,0:T(8,128)}) %all-reduce.4.cloned.1.call-update) | async-done | bytes 106512
  676.5 69.7 %reduce-scatter.11.cloned.1.call-done = bf16[256,2048]{1,0:T(8,128)(2,1)} async-done(((bf16[2048,2048]{1,0:T(8,128)(2,1)}), bf16[256,2048]{1,0:T(8,128)(2,1)}) %reduce-scatter.11.cloned.1.call-update) | async-done | bytes 1048592 | tf_op jit(solution)/shard_map/reduce_scatter | solution.py:146
  746.2 2.8 convert_element_type.367
  749.0 72.4 %reduce-scatter.9.cloned.1.call-done = bf16[256,2048]{1,0:T(8,128)(2,1)} async-done(((bf16[2048,2048]{1,0:T(8,128)(2,1)}), bf16[256,2048]{1,0:T(8,128)(2,1)}) %reduce-scatter.9.cloned.1.call-update) | async-done | bytes 1048592 | tf_op jit(solution)/shard_map/reduce_scatter | solution.py:146
  821.3 4.8 all-to-all-start.3
  829.5 22.3 %all-to-all-done.3 = bf16[4,64,2048]{2,1,0:T(8,128)(2,1)S(1)} async-done(((bf16[4,64,2048]{2,1,0:T(8,128)(2,1)}), bf16[4,64,2048]{2,1,0:T(8,128)(2,1)S(1)}, u32[]{:S(2)}, u32[]{:S(2)}) %all-to-all-start.3) | async-done | bytes 1048608 | tf_op jit(solution)/shard_map/all_to_all | solution.py:150
  853.4 2.1 reshape.449
  (418 shorter events, 69.7 us)
Async XLA Ops:
  7.2 154.6 %all-gather.15.cloned.1.call-start = ((), (), s32[]{:S(2)}) async-start(), calls=%async_computation.15 | async-start | bytes 2359296 | tf_op jit(solution)/shard_map/all_gather | solution.py:124
  7.2 1.6 collective-permute-start.3
  9.6 154.7 %all-gather.9.cloned.1.call-start = ((), (), s32[]{:S(2)}) async-start(), calls=%async_computation.8 | async-start | bytes 7077888 | tf_op jit(solution)/shard_map/all_gather | solution.py:142
  13.2 36.0 %copy-start.41 = (bf16[64,8192]{1,0:T(8,128)(2,1)S(1)}, bf16[64,8192]{1,0:T(8,128)(2,1)}, u32[]{:S(2)}) copy-start(bf16[64,8192]{1,0:T(8,128)(2,1)} %param.31) | copy-start | bytes 3145732
  49.1 221.3 %all-gather.11.cloned.1.call-start = ((), (), s32[]{:S(2)}) async-start(), calls=%async_computation.9 | async-start | bytes 9437184 | tf_op jit(solution)/shard_map/all_gather | solution.py:142
  50.0 29.4 %copy-start.2 = (bf16[1,128,2048]{2,1,0:T(8,128)(2,1)S(1)}, bf16[1,128,2048]{2,1,0:T(8,128)(2,1)}, u32[]{:S(2)}) copy-start(bf16[1,128,2048]{2,1,0:T(8,128)(2,1)} %param.18) | copy-start | bytes 1572868
  50.0 29.7 %copy-start.72 = (bf16[64]{0:T(256)(128)(2,1)S(1)}, bf16[64]{0:T(256)(128)(2,1)}, u32[]{:S(2)}) copy-start(bf16[64]{0:T(256)(128)(2,1)} %param.23) | copy-start | bytes 388
  50.0 29.7 %copy-start.73 = (bf16[64]{0:T(256)(128)(2,1)S(1)}, bf16[64]{0:T(256)(128)(2,1)}, u32[]{:S(2)}) copy-start(bf16[64]{0:T(256)(128)(2,1)} %param.24) | copy-start | bytes 388
  50.0 29.7 %copy-start.74 = (bf16[128]{0:T(256)(128)(2,1)S(1)}, bf16[128]{0:T(256)(128)(2,1)}, u32[]{:S(2)}) copy-start(bf16[128]{0:T(256)(128)(2,1)} %param.26) | copy-start | bytes 772
  50.1 29.7 %copy-start.75 = (bf16[64]{0:T(256)(128)(2,1)S(1)}, bf16[64]{0:T(256)(128)(2,1)}, u32[]{:S(2)}) copy-start(bf16[64]{0:T(256)(128)(2,1)} %param.28) | copy-start | bytes 388
  50.1 29.6 %copy-start.76 = (bf16[64]{0:T(256)(128)(2,1)S(1)}, bf16[64]{0:T(256)(128)(2,1)}, u32[]{:S(2)}) copy-start(bf16[64]{0:T(256)(128)(2,1)} %param.29) | copy-start | bytes 388
  50.1 29.6 %copy-start.77 = (bf16[64]{0:T(256)(128)(2,1)S(1)}, bf16[64]{0:T(256)(128)(2,1)}, u32[]{:S(2)}) copy-start(bf16[64]{0:T(256)(128)(2,1)} %param.30) | copy-start | bytes 388
  50.1 29.6 %copy-start.78 = (bf16[256]{0:T(256)(128)(2,1)S(1)}, bf16[256]{0:T(256)(128)(2,1)}, u32[]{:S(2)}) copy-start(bf16[256]{0:T(256)(128)(2,1)} %param.32) | copy-start | bytes 1540
  50.1 29.6 %copy-start.79 = (bf16[64]{0:T(256)(128)(2,1)S(1)}, bf16[64]{0:T(256)(128)(2,1)}, u32[]{:S(2)}) copy-start(bf16[64]{0:T(256)(128)(2,1)} %param.34) | copy-start | bytes 388
  50.1 29.6 %copy-start.80 = (bf16[64]{0:T(256)(128)(2,1)S(1)}, bf16[64]{0:T(256)(128)(2,1)}, u32[]{:S(2)}) copy-start(bf16[64]{0:T(256)(128)(2,1)} %param.35) | copy-start | bytes 388
  50.1 70.9 %copy-start.69 = (s32[1,128]{1,0:T(1,128)S(1)}, s32[1,128]{1,0:T(1,128)}, u32[]{:S(2)}) copy-start(s32[1,128]{1,0:T(1,128)} %param.22) | copy-start | bytes 1540
  50.1 70.9 %copy-start.70 = (s32[1,128]{1,0:T(1,128)S(1)}, s32[1,128]{1,0:T(1,128)}, u32[]{:S(2)}) copy-start(s32[1,128]{1,0:T(1,128)} %param.21) | copy-start | bytes 1540
  50.2 70.9 %copy-start.71 = (s32[1,128]{1,0:T(1,128)S(1)}, s32[1,128]{1,0:T(1,128)}, u32[]{:S(2)}) copy-start(s32[1,128]{1,0:T(1,128)} %param.20) | copy-start | bytes 1540
  78.8 197.9 %all-gather.13.cloned.1.call-start = ((), (), s32[]{:S(2)}) async-start(), calls=%async_computation.10 | async-start | bytes 9437184 | tf_op jit(solution)/shard_map/all_gather | solution.py:142
  79.4 440.5 %reduce-scatter.5.cloned.1.call-start = ((), (), s32[]{:S(2)}) async-start(), calls=%async_computation.11 | async-start | bytes 7077888 | tf_op jit(solution)/shard_map/reduce_scatter | solution.py:146
  79.4 55.0 %collective-permute-start = (bf16[128,2048]{1,0:T(8,128)(2,1)S(1)}, bf16[128,2048]{1,0:T(8,128)(2,1)S(1)}, u32[]{:S(2)}, u32[]{:S(2)}) collective-permute-start(bf16[128,2048]{1,0:T(8,128)(2,1)S(1)} %bitcast.375), channel_id=1, source_target_pairs={{0,1},{1,2},{2,3},{3,0},{4,5},{5,6},{6,7},{7,4},{8,9},{9,10},{10,1... | collective-permute-start | bytes 1572872 | tf_op jit(solution)/shard_map/ppermute | solution.py:51
  133.8 28.1 %copy-start.65 = (f32[128]{0:T(128)}, f32[128]{0:T(128)S(1)}, u32[]{:S(2)}) copy-start(f32[128]{0:T(128)S(1)} %broadcast_multiply_fusion.8) | copy-start | bytes 1540
  134.1 27.8 %copy-start.67 = (f32[128]{0:T(128)}, f32[128]{0:T(128)S(1)}, u32[]{:S(2)}) copy-start(f32[128]{0:T(128)S(1)} %add_rsqrt_fusion.4) | copy-start | bytes 1540
  134.5 13.0 %collective-permute-start.1 = (bf16[128,2048]{1,0:T(8,128)(2,1)S(1)}, bf16[128,2048]{1,0:T(8,128)(2,1)S(1)}, u32[]{:S(2)}, u32[]{:S(2)}) collective-permute-start(bf16[128,2048]{1,0:T(8,128)(2,1)S(1)} %collective-permute-done), channel_id=1, source_target_pairs={{0,1},{1,2},{2,3},{3,0},{4,5},{5,6},{6,7},{7,4},{8,9},{9,10},{10,1... | collective-permute-start | bytes 1572872 | tf_op jit(solution)/shard_map/ppermute | solution.py:51
  147.4 12.2 %collective-permute-start.2 = (bf16[128,2048]{1,0:T(8,128)(2,1)S(1)}, bf16[128,2048]{1,0:T(8,128)(2,1)S(1)}, u32[]{:S(2)}, u32[]{:S(2)}) collective-permute-start(bf16[128,2048]{1,0:T(8,128)(2,1)S(1)} %collective-permute-done.1), channel_id=1, source_target_pairs={{0,1},{1,2},{2,3},{3,0},{4,5},{5,6},{6,7},{7,4},{8,9},{9,10},{10,1... | collective-permute-start | bytes 1572872 | tf_op jit(solution)/shard_map/ppermute | solution.py:51
  182.7 25.6 %copy-start.62 = (f32[32,64]{1,0:T(8,128)S(1)}, f32[32,64]{1,0:T(8,128)}, u32[]{:S(2)}) copy-start(f32[32,64]{1,0:T(8,128)} %get-tuple-element.78) | copy-start | bytes 24580
  182.7 25.7 %copy-start.61 = (f32[32,64]{1,0:T(8,128)S(1)}, f32[32,64]{1,0:T(8,128)}, u32[]{:S(2)}) copy-start(f32[32,64]{1,0:T(8,128)} %get-tuple-element.74) | copy-start | bytes 24580
  182.7 25.7 %copy-start.60 = (f32[32,64]{1,0:T(8,128)S(1)}, f32[32,64]{1,0:T(8,128)}, u32[]{:S(2)}) copy-start(f32[32,64]{1,0:T(8,128)} %get-tuple-element.75) | copy-start | bytes 24580
  182.7 25.8 %copy-start.59 = (f32[32,64]{1,0:T(8,128)S(1)}, f32[32,64]{1,0:T(8,128)}, u32[]{:S(2)}) copy-start(f32[32,64]{1,0:T(8,128)} %get-tuple-element.76) | copy-start | bytes 24580
  183.2 11.6 %collective-permute-start.4 = (bf16[128,2048]{1,0:T(8,128)(2,1)S(1)}, bf16[128,2048]{1,0:T(8,128)(2,1)S(1)}, u32[]{:S(2)}, u32[]{:S(2)}) collective-permute-start(bf16[128,2048]{1,0:T(8,128)(2,1)S(1)} %convolution_convert_fusion.6), channel_id=1, source_target_pairs={{0,1},{1,2},{2,3},{3,0},{4,5},{5,6},{6,7},{7,4},{8,9},{9,10},{10,1... | collective-permute-start | bytes 1572872 | tf_op jit(solution)/shard_map/ppermute | solution.py:59
  195.3 12.4 %collective-permute-start.5 = (bf16[128,2048]{1,0:T(8,128)(2,1)S(1)}, bf16[128,2048]{1,0:T(8,128)(2,1)S(1)}, u32[]{:S(2)}, u32[]{:S(2)}) collective-permute-start(bf16[128,2048]{1,0:T(8,128)(2,1)S(1)} %add_convert_fusion.11), channel_id=1, source_target_pairs={{0,1},{1,2},{2,3},{3,0},{4,5},{5,6},{6,7},{7,4},{8,9},{9,10},{10,1... | collective-permute-start | bytes 1572872 | tf_op jit(solution)/shard_map/ppermute | solution.py:59
  208.2 39.4 %copy-start.64 = (s32[4,3,128]{2,1,0:T(4,128)S(1)}, s32[4,3,128]{2,1,0:T(4,128)}, u32[]{:S(2)}) copy-start(s32[4,3,128]{2,1,0:T(4,128)} %copy-done.63) | copy-start | bytes 18436
  208.2 16.7 %collective-permute-start.6 = (bf16[128,2048]{1,0:T(8,128)(2,1)S(1)}, bf16[128,2048]{1,0:T(8,128)(2,1)S(1)}, u32[]{:S(2)}, u32[]{:S(2)}) collective-permute-start(bf16[128,2048]{1,0:T(8,128)(2,1)S(1)} %add_convert_fusion.10), channel_id=1, source_target_pairs={{0,1},{1,2},{2,3},{3,0},{4,5},{5,6},{6,7},{7,4},{8,9},{9,10},{10,1... | collective-permute-start | bytes 1572872 | tf_op jit(solution)/shard_map/ppermute | solution.py:59
  208.3 28.0 %collective-permute-start.13 = (bf16[128,2048]{1,0:T(8,128)(2,1)}, bf16[128,2048]{1,0:T(8,128)(2,1)}, u32[]{:S(2)}, u32[]{:S(2)}) collective-permute-start(bf16[128,2048]{1,0:T(8,128)(2,1)} %bitcast.44), channel_id=1, source_target_pairs={{0,1},{1,2},{2,3},{3,0},{4,5},{5,6},{6,7},{7,4},{8,9},{9,10},{10,1... | collective-permute-start | bytes 1572872 | tf_op jit(solution)/shard_map/ppermute | solution.py:51
  228.9 18.6 %collective-permute-start.7 = (bf16[128,2048]{1,0:T(8,128)(2,1)S(1)}, bf16[128,2048]{1,0:T(8,128)(2,1)}, u32[]{:S(2)}, u32[]{:S(2)}) collective-permute-start(bf16[128,2048]{1,0:T(8,128)(2,1)S(1)} %add_convert_fusion.9), channel_id=1, source_target_pairs={{0,1},{1,2},{2,3},{3,0},{4,5},{5,6},{6,7},{7,4},{8,9},{9,10},{10,1... | collective-permute-start | bytes 1572872 | tf_op jit(solution)/shard_map/ppermute | solution.py:51
  236.2 22.5 %collective-permute-start.15 = (bf16[128,2048]{1,0:T(8,128)(2,1)}, bf16[128,2048]{1,0:T(8,128)(2,1)}, u32[]{:S(2)}, u32[]{:S(2)}) collective-permute-start(bf16[128,2048]{1,0:T(8,128)(2,1)} %collective-permute-done.13), channel_id=1, source_target_pairs={{0,1},{1,2},{2,3},{3,0},{4,5},{5,6},{6,7},{7,4},{8,9},{9,10},{10,1... | collective-permute-start | bytes 1572872 | tf_op jit(solution)/shard_map/ppermute | solution.py:51
  247.5 22.5 %collective-permute-start.9 = (bf16[128,2048]{1,0:T(8,128)(2,1)}, bf16[128,2048]{1,0:T(8,128)(2,1)}, u32[]{:S(2)}, u32[]{:S(2)}) collective-permute-start(bf16[128,2048]{1,0:T(8,128)(2,1)} %collective-permute-done.7), channel_id=1, source_target_pairs={{0,1},{1,2},{2,3},{3,0},{4,5},{5,6},{6,7},{7,4},{8,9},{9,10},{10,1... | collective-permute-start | bytes 1572872 | tf_op jit(solution)/shard_map/ppermute | solution.py:51
  258.7 61.1 %collective-permute-start.17 = (bf16[128,2048]{1,0:T(8,128)(2,1)}, bf16[128,2048]{1,0:T(8,128)(2,1)}, u32[]{:S(2)}, u32[]{:S(2)}) collective-permute-start(bf16[128,2048]{1,0:T(8,128)(2,1)} %collective-permute-done.15), channel_id=1, source_target_pairs={{0,1},{1,2},{2,3},{3,0},{4,5},{5,6},{6,7},{7,4},{8,9},{9,10},{10,1... | collective-permute-start | bytes 1572872 | tf_op jit(solution)/shard_map/ppermute | solution.py:51
  269.9 20.8 %collective-permute-start.11 = (bf16[128,2048]{1,0:T(8,128)(2,1)}, bf16[128,2048]{1,0:T(8,128)(2,1)}, u32[]{:S(2)}, u32[]{:S(2)}) collective-permute-start(bf16[128,2048]{1,0:T(8,128)(2,1)} %collective-permute-done.9), channel_id=1, source_target_pairs={{0,1},{1,2},{2,3},{3,0},{4,5},{5,6},{6,7},{7,4},{8,9},{9,10},{10,1... | collective-permute-start | bytes 1572872 | tf_op jit(solution)/shard_map/ppermute | solution.py:51
  281.7 15.8 %collective-permute-start.8 = (bf16[128,2048]{1,0:T(8,128)(2,1)S(1)}, bf16[128,2048]{1,0:T(8,128)(2,1)S(1)}, u32[]{:S(2)}, u32[]{:S(2)}) collective-permute-start(bf16[128,2048]{1,0:T(8,128)(2,1)S(1)} %get-tuple-element.121), channel_id=1, source_target_pairs={{0,1},{1,2},{2,3},{3,0},{4,5},{5,6},{6,7},{7,4},{8,9},{9,10},{10,1... | collective-permute-start | bytes 1572872 | tf_op jit(solution)/shard_map/ppermute | solution.py:59
  298.8 11.2 %collective-permute-start.10 = (bf16[128,2048]{1,0:T(8,128)(2,1)S(1)}, bf16[128,2048]{1,0:T(8,128)(2,1)S(1)}, u32[]{:S(2)}, u32[]{:S(2)}) collective-permute-start(bf16[128,2048]{1,0:T(8,128)(2,1)S(1)} %get-tuple-element.123), channel_id=1, source_target_pairs={{0,1},{1,2},{2,3},{3,0},{4,5},{5,6},{6,7},{7,4},{8,9},{9,10},{10,1... | collective-permute-start | bytes 1572872 | tf_op jit(solution)/shard_map/ppermute | solution.py:59
  333.3 13.9 %collective-permute-start.14 = (bf16[128,2048]{1,0:T(8,128)(2,1)S(1)}, bf16[128,2048]{1,0:T(8,128)(2,1)S(1)}, u32[]{:S(2)}, u32[]{:S(2)}) collective-permute-start(bf16[128,2048]{1,0:T(8,128)(2,1)S(1)} %convolution_convert_fusion.4), channel_id=1, source_target_pairs={{0,1},{1,2},{2,3},{3,0},{4,5},{5,6},{6,7},{7,4},{8,9},{9,10},{10,1... | collective-permute-start | bytes 1572872 | tf_op jit(solution)/shard_map/ppermute | solution.py:59
  335.4 34.1 %collective-permute-start.12 = (bf16[128,2048]{1,0:T(8,128)(2,1)S(1)}, bf16[128,2048]{1,0:T(8,128)(2,1)S(1)}, u32[]{:S(2)}, u32[]{:S(2)}) collective-permute-start(bf16[128,2048]{1,0:T(8,128)(2,1)S(1)} %copy-done.47), channel_id=1, source_target_pairs={{0,1},{1,2},{2,3},{3,0},{4,5},{5,6},{6,7},{7,4},{8,9},{9,10},{10,1... | collective-permute-start | bytes 1572872 | tf_op jit(solution)/shard_map/ppermute | solution.py:59
  338.8 27.8 %copy-start.19 = (bf16[128,2048]{1,0:T(8,128)(2,1)}, bf16[128,2048]{1,0:T(8,128)(2,1)S(1)}, u32[]{:S(2)}) copy-start(bf16[128,2048]{1,0:T(8,128)(2,1)S(1)} %fusion.106) | copy-start | bytes 1572868
  350.1 14.6 %collective-permute-start.16 = (bf16[128,2048]{1,0:T(8,128)(2,1)S(1)}, bf16[128,2048]{1,0:T(8,128)(2,1)S(1)}, u32[]{:S(2)}, u32[]{:S(2)}) collective-permute-start(bf16[128,2048]{1,0:T(8,128)(2,1)S(1)} %add_convert_fusion.4), channel_id=1, source_target_pairs={{0,1},{1,2},{2,3},{3,0},{4,5},{5,6},{6,7},{7,4},{8,9},{9,10},{10,1... | collective-permute-start | bytes 1572872 | tf_op jit(solution)/shard_map/ppermute | solution.py:59
  364.9 11.5 %collective-permute-start.18 = (bf16[128,2048]{1,0:T(8,128)(2,1)S(1)}, bf16[128,2048]{1,0:T(8,128)(2,1)S(1)}, u32[]{:S(2)}, u32[]{:S(2)}) collective-permute-start(bf16[128,2048]{1,0:T(8,128)(2,1)S(1)} %add_convert_fusion.2), channel_id=1, source_target_pairs={{0,1},{1,2},{2,3},{3,0},{4,5},{5,6},{6,7},{7,4},{8,9},{9,10},{10,1... | collective-permute-start | bytes 1572872 | tf_op jit(solution)/shard_map/ppermute | solution.py:59
  380.6 16.6 %collective-permute-start.19 = (bf16[128,2048]{1,0:T(8,128)(2,1)S(1)}, bf16[128,2048]{1,0:T(8,128)(2,1)S(1)}, u32[]{:S(2)}, u32[]{:S(2)}) collective-permute-start(bf16[128,2048]{1,0:T(8,128)(2,1)S(1)} %get-tuple-element.34), channel_id=1, source_target_pairs={{0,1},{1,2},{2,3},{3,0},{4,5},{5,6},{6,7},{7,4},{8,9},{9,10},{10,1... | collective-permute-start | bytes 1572872 | tf_op jit(solution)/shard_map/ppermute | solution.py:51
  397.1 15.7 %collective-permute-start.20 = (bf16[128,2048]{1,0:T(8,128)(2,1)S(1)}, bf16[128,2048]{1,0:T(8,128)(2,1)S(1)}, u32[]{:S(2)}, u32[]{:S(2)}) collective-permute-start(bf16[128,2048]{1,0:T(8,128)(2,1)S(1)} %collective-permute-done.19), channel_id=1, source_target_pairs={{0,1},{1,2},{2,3},{3,0},{4,5},{5,6},{6,7},{7,4},{8,9},{9,10},{10,1... | collective-permute-start | bytes 1572872 | tf_op jit(solution)/shard_map/ppermute | solution.py:51
  398.0 27.5 %copy-start.6 = (f32[4,512,512]{1,2,0:T(8,128)S(1)}, f32[4,512,512]{1,2,0:T(8,128)}, u32[]{:S(2)}) copy-start(f32[4,512,512]{1,2,0:T(8,128)} %get-tuple-element.112) | copy-start | bytes 12582916
  412.9 11.0 %collective-permute-start.21 = (bf16[128,2048]{1,0:T(8,128)(2,1)S(1)}, bf16[128,2048]{1,0:T(8,128)(2,1)S(1)}, u32[]{:S(2)}, u32[]{:S(2)}) collective-permute-start(bf16[128,2048]{1,0:T(8,128)(2,1)S(1)} %collective-permute-done.20), channel_id=1, source_target_pairs={{0,1},{1,2},{2,3},{3,0},{4,5},{5,6},{6,7},{7,4},{8,9},{9,10},{10,1... | collective-permute-start | bytes 1572872 | tf_op jit(solution)/shard_map/ppermute | solution.py:51
  435.8 108.1 %reduce-scatter.7.cloned.1.call-start = ((), (), s32[]{:S(2)}) async-start(), calls=%async_computation.12 | async-start | bytes 2359296 | tf_op jit(solution)/shard_map/reduce_scatter | solution.py:146
  441.0 229.7 %all-reduce.4.cloned.1.call-start = ((), (), s32[]{:S(2)}) async-start(), calls=%async_computation.16 | async-start | bytes 229376
  441.0 25.0 %slice-start.6 = ((s8[6291456]{0:T(1024)(128)(4,1)}), s8[4194304]{0:T(1024)(128)(4,1)S(1)}, s32[]{:S(2)}) async-start(s8[6291456]{0:T(1024)(128)(4,1)} %bitcast.365), calls=%async_computation.23 | async-start | bytes 8388608
  446.7 13.9 %collective-permute-start.22 = (bf16[128,2048]{1,0:T(8,128)(2,1)S(1)}, bf16[128,2048]{1,0:T(8,128)(2,1)S(1)}, u32[]{:S(2)}, u32[]{:S(2)}) collective-permute-start(bf16[128,2048]{1,0:T(8,128)(2,1)S(1)} %convolution_convert_fusion.5), channel_id=1, source_target_pairs={{0,1},{1,2},{2,3},{3,0},{4,5},{5,6},{6,7},{7,4},{8,9},{9,10},{10,1... | collective-permute-start | bytes 1572872 | tf_op jit(solution)/shard_map/ppermute | solution.py:59
  466.0 14.0 %collective-permute-start.23 = (bf16[128,2048]{1,0:T(8,128)(2,1)S(1)}, bf16[128,2048]{1,0:T(8,128)(2,1)S(1)}, u32[]{:S(2)}, u32[]{:S(2)}) collective-permute-start(bf16[128,2048]{1,0:T(8,128)(2,1)S(1)} %add_convert_fusion.1), channel_id=1, source_target_pairs={{0,1},{1,2},{2,3},{3,0},{4,5},{5,6},{6,7},{7,4},{8,9},{9,10},{10,1... | collective-permute-start | bytes 1572872 | tf_op jit(solution)/shard_map/ppermute | solution.py:59
  468.2 23.9 %copy-start.3 = (bf16[1,128,2048]{2,1,0:T(8,128)(2,1)S(1)}, bf16[1,128,2048]{2,1,0:T(8,128)(2,1)}, u32[]{:S(2)}) copy-start(bf16[1,128,2048]{2,1,0:T(8,128)(2,1)} %param.18) | copy-start | bytes 1572868
  480.9 11.3 %collective-permute-start.24 = (bf16[128,2048]{1,0:T(8,128)(2,1)}, bf16[128,2048]{1,0:T(8,128)(2,1)}, u32[]{:S(2)}, u32[]{:S(2)}) collective-permute-start(bf16[128,2048]{1,0:T(8,128)(2,1)} %add_convert_fusion), channel_id=1, source_target_pairs={{0,1},{1,2},{2,3},{3,0},{4,5},{5,6},{6,7},{7,4},{8,9},{9,10},{10,1... | collective-permute-start | bytes 1572872 | tf_op jit(solution)/shard_map/ppermute | solution.py:59
  499.3 246.9 %reduce-scatter.11.cloned.1.call-start = ((), (), s32[]{:S(2)}) async-start(), calls=%async_computation.14 | async-start | bytes 9437184 | tf_op jit(solution)/shard_map/reduce_scatter | solution.py:146
  509.2 312.1 %reduce-scatter.9.cloned.1.call-start = ((), (), s32[]{:S(2)}) async-start(), calls=%async_computation.13 | async-start | bytes 9437184 | tf_op jit(solution)/shard_map/reduce_scatter | solution.py:146
  519.3 28.1 %copy-start.7 = (f32[128,2048]{1,0:T(8,128)S(1)}, f32[128,2048]{1,0:T(8,128)}, u32[]{:S(2)}) copy-start(f32[128,2048]{1,0:T(8,128)} %get-tuple-element.35) | copy-start | bytes 3145732
  519.3 28.1 %copy-start.42 = (f32[128,2048]{1,0:T(8,128)S(1)}, f32[128,2048]{1,0:T(8,128)}, u32[]{:S(2)}) copy-start(f32[128,2048]{1,0:T(8,128)} %get-tuple-element.127) | copy-start | bytes 3145732
  519.9 301.5 %all-to-all-start.2 = ((bf16[4,64,1536]{2,1,0:T(8,128)(2,1)}), bf16[4,64,1536]{2,1,0:T(8,128)(2,1)S(1)}, u32[]{:S(2)}, u32[]{:S(2)}) async-start(bf16[4,64,1536]{2,1,0:T(8,128)(2,1)} %bitcast.403), calls=%async_computation.3 | async-start | bytes 1572864 | tf_op jit(solution)/shard_map/all_to_all | solution.py:150
  543.8 130.9 %collective-permute-start.25 = (bf16[64,2048]{1,0:T(8,128)(2,1)}, bf16[64,2048]{1,0:T(8,128)(2,1)}, u32[]{:S(2)}, u32[]{:S(2)}) collective-permute-start(bf16[64,2048]{1,0:T(8,128)(2,1)} %reduce-scatter.7.cloned.1.call-done), channel_id=1, source_target_pairs={{0,0},{16,1},{2,2},{18,3},{4,4},{20,5},{6,6},{22,7},{8,8},{24,9},{... | collective-permute-start | bytes 786440 | tf_op jit(solution)/shard_map/ppermute | solution.py:138
  821.3 30.5 %all-to-all-start.3 = ((bf16[4,64,2048]{2,1,0:T(8,128)(2,1)}), bf16[4,64,2048]{2,1,0:T(8,128)(2,1)S(1)}, u32[]{:S(2)}, u32[]{:S(2)}) async-start(bf16[4,64,2048]{2,1,0:T(8,128)(2,1)} %bitcast.391), calls=%async_computation.6 | async-start | bytes 2097152 | tf_op jit(solution)/shard_map/all_to_all | solution.py:150
  (62 other events, 472.6 us)
Sparse Core Ops, SparseCore 0:
  10.5 38.2 all-gather.14
  50.7 46.1 all-gather.8
  98.7 55.0 all-gather.10
  155.6 54.4 all-gather.12
  435.9 62.5 reduce-scatter.4
  502.6 41.2 reduce-scatter.6
  550.0 120.6 all-reduce.3
  674.1 71.9 reduce-scatter.10
  750.0 71.2 reduce-scatter.8

commit v2 on v1

v2 whole, which is shorter than its diff:
```python
from functools import partial

import jax
import jax.numpy as jnp
from jax import lax
from jax.experimental import pallas as pl
from jax.experimental.pallas import tpu as pltpu
from jax.sharding import PartitionSpec as P

HEADS = 16
EPSILON = 1e-05
MASKED = -1e30
LOW = jnp.bfloat16
WIDE = jnp.float32
EVERY = ("dp", "seq")


def product(left, right):
    return jnp.dot(left, right, preferred_element_type=WIDE)


def inner_rows(left, right):
    return jnp.einsum("ta,tb->ab", left, right, preferred_element_type=WIDE)


def against_rows(left, right):
    return jnp.einsum("tb,ab->ta", left, right, preferred_element_type=WIDE)


def normalize_parts(field, gain, shift):
    center = field - jnp.mean(field, axis=-1, keepdims=True)
    spread = jnp.mean(center * center, axis=-1, keepdims=True)
    inverse = lax.rsqrt(spread + EPSILON)
    normal = center * inverse
    return (normal * gain + shift, normal, inverse)


def normalize_back(upstream, normal, inverse, gain):
    scaled = upstream * gain
    mean_scaled = jnp.mean(scaled, axis=-1, keepdims=True)
    mean_cross = jnp.mean(scaled * normal, axis=-1, keepdims=True)
    return inverse * (scaled - mean_scaled - normal * mean_cross)


def ring_next():
    size = lax.axis_size("seq")
    return [(place, (place + 1) % size) for place in range(size)]


def after(value, done):
    return lax.optimization_barrier((value, tuple(done)))[0]


class Task:
    def __init__(self, stages, *operands):
        self.gate = ()
        self.result = None
        self.stages = stages(self, *operands)

    def go(self, gate=()):
        self.gate = tuple(gate)
        return list(next(self.stages, []))

    def finish(self):
        for _ in self.stages:
            pass
        return self.result


def idle(gate):
    return []


def ring_gather(block, flights=(idle,) * 3, use=None, plan=()):
    blocks, results = [block], []
    for k in range(lax.axis_size("seq") - 1):
        moved = lax.ppermute(block, "seq", ring_next())
        done = []
        if use is not None:
            for _ in range(plan[k]):
                results.append(use(len(results), blocks[len(results)]))
                done += jax.tree.leaves(results[-1])
        done += flights[k]((block,))
        block = after(moved, done) if done else moved
        blocks.append(block)
    if use is None:
        return blocks
    while len(results) < len(blocks):
        results.append(use(len(results), blocks[len(results)]))
    return blocks, results


def ring_sum(part, flights=(idle,) * 3):
    total = part(1, ())
    for step, k in enumerate(list(range(2, lax.axis_size("seq"))) + [0]):
        sent = total.astype(LOW)
        moved = lax.ppermute(sent, "seq", ring_next())
        term = part(k, (sent,))
        total = after(moved, [term] + flights[step]((sent,))).astype(WIDE) + term
    return total


def ring_gather_task(task, block):
    task.result = [block]
    for _ in range(lax.axis_size("seq") - 1):
        moved = lax.ppermute(task.result[-1], "seq", ring_next())
        task.result.append(after(moved, task.gate))
        yield [moved]


def ring_sum_task(task, parts):
    total = parts[1]
    for part in parts[2:] + parts[:1]:
        moved = lax.ppermute(total.astype(LOW), "seq", ring_next())
        total = after(moved, task.gate).astype(WIDE) + part
        yield [moved]
    task.result = total


def deal_kernel(pieces, wide, riders, me_ref, from_ref, *refs):
    rider_refs, to_refs, packed = refs[:riders], refs[riders:-1], refs[-1]
    ranks = len(to_refs)
    columns = from_ref.shape[1] // ranks
    if riders:
        packed[...] = jnp.zeros_like(packed)
        row = 0
        for rider_ref in rider_refs:
            lines, width = rider_ref.shape
            packed[row : row + lines, :width] = rider_ref[...].astype(WIDE)
            row += lines
    for shift, to_ref in enumerate(to_refs):
        to = lax.rem(me_ref[0] + shift, ranks)
        for place in range(columns // wide):
            start = pl.multiple_of(pieces(to, place) * wide, wide)
            to_ref[:, place * wide : (place + 1) * wide] = from_ref[:, pl.ds(start, wide)]
        if riders:
            to_ref[:, columns:] = packed[...].astype(to_ref.dtype)


def deal(matrix, pieces, wide, riders=()):
    ranks, me = lax.axis_size("seq"), lax.axis_index("seq")
    rows, columns = matrix.shape
    if wide % 128 == 0:
        each = columns // ranks + (128 if riders else 0)
        return pl.pallas_call(
            partial(deal_kernel, pieces, wide, len(riders)),
            out_shape=[jax.ShapeDtypeStruct((rows, each), matrix.dtype)] * ranks,
            grid_spec=pltpu.PrefetchScalarGridSpec(
                num_scalar_prefetch=1,
                grid=(1,),
                in_specs=[pl.BlockSpec((rows, columns), lambda i, me: (0, 0))]
                + [pl.BlockSpec(rider.shape, lambda i, me: (0, 0)) for rider in riders],
                out_specs=[pl.BlockSpec((rows, each), lambda i, me: (0, 0))] * ranks,
                scratch_shapes=[pltpu.VMEM((rows, 128), WIDE)],
            ),
            name="deal",
        )(me[None], matrix, *riders)
    dealt = jnp.stack(
        [
            jnp.concatenate(
                [
                    matrix[:, pieces(to, place) * wide :][:, :wide]
                    for place in range(columns // ranks // wide)
                ],
                axis=1,
            )
            for to in range(ranks)
        ]
    )
    return [
        lax.dynamic_index_in_dim(dealt, (me + shift) % ranks, 0, keepdims=False)
        for shift in range(ranks)
    ]


def collect_kernel(pieces, wide, me_ref, *refs):
    from_refs, to_ref = refs[:-1], refs[-1]
    ranks = len(from_refs)
    for shift, from_ref in enumerate(from_refs):
        source = lax.rem(me_ref[0] + ranks - shift, ranks)
        for place in range(from_ref.shape[1] // wide):
            start = pl.multiple_of(pieces(source, place) * wide, wide)
            to_ref[:, pl.ds(start, wide)] = from_ref[:, place * wide : (place + 1) * wide].astype(
                to_ref.dtype
            )


def collect(blocks, pieces, wide):
    ranks, me = lax.axis_size("seq"), lax.axis_index("seq")
    rows, columns = blocks[0].shape
    if wide % 128 == 0:
        return pl.pallas_call(
            partial(collect_kernel, pieces, wide),
            out_shape=jax.ShapeDtypeStruct((rows, columns * ranks), WIDE),
            grid_spec=pltpu.PrefetchScalarGridSpec(
                num_scalar_prefetch=1,
                grid=(1,),
                in_specs=[pl.BlockSpec((rows, columns), lambda i, me: (0, 0))] * ranks,
                out_specs=pl.BlockSpec((rows, columns * ranks), lambda i, me: (0, 0)),
            ),
            name="collect",
        )(me[None], *blocks)
    held = by_number(blocks)
    found = {
        pieces(to, place): held[to, :, place * wide : (place + 1) * wide]
        for to in range(ranks)
        for place in range(columns // wide)
    }
    return jnp.concatenate([found[piece] for piece in sorted(found)], axis=1).astype(WIDE)


def place_kernel(sources, to_row_ref, *refs):
    from_refs, (to_ref, held, in_sem, out_sem) = refs[:-4], refs[-4:]
    loads, stores = [], []
    at = 0
    for number, (array, row, rows) in enumerate(sources):
        start = pl.multiple_of(to_row_ref[number], rows)
        piece = held.at[pl.ds(at, rows)]
        loads.append(
            pltpu.make_async_copy(from_refs[array].at[pl.ds(row, rows)], piece, in_sem.at[number])
        )
        stores.append(
            pltpu.make_async_copy(piece, to_ref.at[pl.ds(start, rows)], out_sem.at[number])
        )
        at += rows
    for load in loads:
        load.start()
    for load, store in zip(loads, stores):
        load.wait()
        store.start()
    for store in stores:
        store.wait()


def place_rows(arrays, sources, to_rows):
    total, width = sum(rows for _, _, rows in sources), arrays[0].shape[1]
    count = len(sources)
    if all(rows % 16 == 0 for _, _, rows in sources):
        return pl.pallas_call(
            partial(place_kernel, sources),
            out_shape=jax.ShapeDtypeStruct((total, width), arrays[0].dtype),
            grid_spec=pltpu.PrefetchScalarGridSpec(
                num_scalar_prefetch=1,
                grid=(1,),
                in_specs=[pl.BlockSpec(memory_space=pl.ANY)] * len(arrays),
                out_specs=pl.BlockSpec(memory_space=pl.ANY),
                scratch_shapes=[
                    pltpu.VMEM((total, width), arrays[0].dtype),
                    pltpu.SemaphoreType.DMA((count,)),
                    pltpu.SemaphoreType.DMA((count,)),
                ],
            ),
            compiler_params=pltpu.CompilerParams(
                vmem_limit_bytes=total * width * 2 + 4 * 2**20
            ),
            name="place_rows",
        )(to_rows, *arrays)
    whole = jnp.zeros((total, width), arrays[0].dtype)
    for number, (array, row, rows) in enumerate(sources):
        whole = lax.dynamic_update_slice_in_dim(
            whole, arrays[array][row : row + rows], to_rows[number], 0
        )
    return whole


def to_ring(table):
    size = lax.axis_size("seq")
    me = lax.axis_index("seq")
    return jnp.stack(
        [lax.dynamic_index_in_dim(table, (me - k) % size, 0, keepdims=False) for k in range(size)]
    )


def head_of(rank, place):
    groups, ranks = lax.axis_size("dp"), lax.axis_size("seq")
    blocks = groups * ranks // HEADS
    if blocks <= ranks:
        held = groups // blocks
        return (rank % blocks * held + place) * (ranks // blocks) + rank // blocks
    return place * ranks + rank


def heads_of():
    ranks = lax.axis_size("seq")
    return [[head_of(rank, place) for place in range(HEADS // ranks)] for rank in range(ranks)]


def head_pieces(rank, place):
    held = HEADS // lax.axis_size("seq")
    return place // held * HEADS + head_of(rank, place % held)


def hidden_pieces(rank, place):
    return place * lax.axis_size("seq") + rank


def own_heads():
    numbers = jnp.array(heads_of())
    mine = lax.dynamic_index_in_dim(numbers, lax.axis_index("seq"), 0, keepdims=False)
    return (mine[:, None] == jnp.arange(HEADS)[None, :]).astype(WIDE)


def exact(left, right):
    return jnp.dot(left, right, precision=lax.Precision.HIGHEST, preferred_element_type=WIDE)


def out_route():
    groups, ranks = lax.axis_size("dp"), lax.axis_size("seq")
    blocks = groups * ranks // HEADS
    route = []
    for group in range(groups):
        for rank in range(ranks):
            if blocks <= ranks:
                held = groups // blocks
                high, low = divmod(group, held)
                pair, part = divmod(rank, blocks)
                target = (part * held + low, pair * blocks + high)
            else:
                span = blocks // ranks
                head, extra = divmod(group, span)
                high, low = divmod(head, ranks)
                target = ((high * ranks + rank) * span + extra, low)
            route.append((group * ranks + rank, target[0] * ranks + target[1]))
    return route


def out_parts():
    groups, ranks = lax.axis_size("dp"), lax.axis_size("seq")
    blocks = groups * ranks // HEADS
    if blocks <= ranks:
        return ((blocks, groups // blocks), (1, 0))
    return ((HEADS // ranks, ranks, blocks // ranks), (0, 2, 1))


def out_gather(moved):
    whole = lax.all_gather(moved, "dp", axis=0, tiled=False)
    split, order = out_parts()
    tail = tuple(range(len(split), len(split) + 2))
    return whole.reshape(split + moved.shape).transpose(order + tail).reshape(-1, moved.shape[1])


def gather_groups(block):
    return lax.all_gather(block, "dp", axis=0, tiled=True)


def swap_bit(block, axis, bit):
    return lax.ppermute(
        block, axis, [(place, place ^ (1 << bit)) for place in range(lax.axis_size(axis))]
    )


def bits_of(axis):
    return range(lax.axis_size(axis).bit_length() - 1)


def pair_kernel(lefts, rights, kept, me_ref, *refs):
    left_refs, right_refs, rest = refs[:lefts], refs[lefts : lefts + rights], refs[lefts + rights :]
    left, right = joined(left_refs), joined(right_refs)
    total = lax.dot_general(left, right, (((0,), (0,)), ((), ())), preferred_element_type=WIDE)
    if not kept:
        rest[0][...] = total.astype(LOW)
        return
    total = (total + rest[0][...].astype(WIDE)).astype(LOW)
    half = total.shape[1] // 2
    for number in range(4):

        @pl.when(pl.program_id(0) == number)
        def _():
            rest[1 + number][...] = total[:, :half]
            rest[5 + number][...] = total[:, half:]


def pair_product(lefts, rights, rows, got=None):
    groups, me = lax.axis_size("dp"), lax.axis_index("dp")
    pairs, width = groups // 2, rights[0].shape[1]
    kept = got is not None

    def left_block(number, me):
        side = lax.rem(me[0], 2)
        return (0, (me[0] // 2 ^ number) * 2 + (side if kept else 1 - side))

    in_specs = [pl.BlockSpec((left.shape[0], rows), left_block) for left in lefts]
    once = pl.Buffered(1)
    in_specs += [
        pl.BlockSpec(right.shape, lambda number, me: (0, 0), pipeline_mode=once) for right in rights
    ]
    block = pl.BlockSpec((rows, width), lambda number, me: (number, 0))
    if kept:
        in_specs.append(block)
        shape = (rows, width // 2)
        out_specs = [pl.BlockSpec(shape, lambda number, me: (0, 0), pipeline_mode=once)] * (2 * pairs)
        out_shape = [pltpu.HBM(shape, LOW)] * (2 * pairs)
    else:
        out_specs = block
        out_shape = pltpu.HBM((pairs * rows, width), LOW)
    return pl.pallas_call(
        partial(pair_kernel, len(lefts), len(rights), kept),
        out_shape=out_shape,
        grid_spec=pltpu.PrefetchScalarGridSpec(
            num_scalar_prefetch=1, grid=(pairs,), in_specs=in_specs, out_specs=out_specs
        ),
        compiler_params=pltpu.CompilerParams(vmem_limit_bytes=18 * 2**20),
        cost_estimate=pl.CostEstimate(
            flops=4 * pairs * rows * width * sum(left.shape[0] for left in lefts),
            bytes_accessed=4 * pairs * rows * width,
            transcendentals=0,
        ),
        name="pair_product",
    )(me[None], *lefts, *rights, *([got] if kept else []))


GELU_SCALE = (2 / jnp.pi) ** 0.5
GELU_CUBE = 0.044715
PARAMETERS = dict(vmem_limit_bytes=16 * 2**20)


def gelu_parts(value):
    square = value * value
    bent = jnp.tanh(GELU_SCALE * value * (1 + GELU_CUBE * square))
    slope = 0.5 * (1 + bent) + 0.5 * value * (1 - bent * bent) * GELU_SCALE * (
        1 + 3 * GELU_CUBE * square
    )
    return 0.5 * value * (1 + bent), slope


def whole_block(array):
    return pl.BlockSpec(array.shape, lambda number: (0, 0), pipeline_mode=pl.Buffered(1))


def column_block(rows, wide):
    return pl.BlockSpec((rows, wide), lambda number: (0, number))


def joined(refs):
    return jnp.concatenate([ref[...] for ref in refs])


def estimate(rows, depth, width):
    return pl.CostEstimate(
        flops=4 * rows * depth * width, bytes_accessed=2 * depth * width, transcendentals=0
    )


def project_kernel(left_ref, weight_ref, bias_ref, to_ref):
    total = jnp.dot(left_ref[...], weight_ref[...], preferred_element_type=WIDE)
    to_ref[...] = (total + bias_ref[...]).astype(to_ref.dtype)


def project(left, weight, bias):
    (rows, depth), width, wide = left.shape, bias.shape[0], 256
    return pl.pallas_call(
        project_kernel,
        out_shape=jax.ShapeDtypeStruct((rows, width), LOW),
        grid=(width // wide,),
        in_specs=[whole_block(left), column_block(depth, wide), column_block(1, wide)],
        out_specs=column_block(rows, wide),
        compiler_params=pltpu.CompilerParams(**PARAMETERS),
        cost_estimate=estimate(rows, depth, width),
        name="project",
    )(left, weight, bias[None])


def upward_kernel(left_ref, weight_ref, bias_ref, upward_ref, active_ref):
    total = jnp.dot(left_ref[...], weight_ref[...], preferred_element_type=WIDE)
    total = total + bias_ref[...]
    upward_ref[...] = total
    active_ref[...] = gelu_parts(total)[0].astype(LOW)


def upward_product(left, weight, bias):
    (rows, depth), width, wide = left.shape, weight.shape[1], 256
    return pl.pallas_call(
        upward_kernel,
        out_shape=[
            jax.ShapeDtypeStruct((rows, width), WIDE),
            jax.ShapeDtypeStruct((rows, width), LOW),
        ],
        grid=(width // wide,),
        in_specs=[whole_block(left), column_block(depth, wide), column_block(1, wide)],
        out_specs=[column_block(rows, wide)] * 2,
        compiler_params=pltpu.CompilerParams(**PARAMETERS),
        cost_estimate=estimate(rows, depth, width),
        name="upward_product",
    )(left, weight, bias[None])


def dense_kernel(lefts, *refs):
    weight_ref, reward_ref, to_ref, reward_to_ref = refs[lefts:]
    total = jnp.dot(joined(refs[:lefts]), weight_ref[...], preferred_element_type=WIDE)
    to_ref[...] = total
    scaled = total * reward_ref[...]
    part = scaled[:, :128]
    for start in range(128, scaled.shape[1], 128):
        part = part + scaled[:, start : start + 128]

    @pl.when(pl.program_id(0) == 0)
    def _():
        reward_to_ref[...] = part

    @pl.when(pl.program_id(0) > 0)
    def _():
        reward_to_ref[...] += part


def dense_product(lefts, weight, reward):
    (depth, width), wide = weight.shape, 256
    rows = sum(left.shape[0] for left in lefts)
    return pl.pallas_call(
        partial(dense_kernel, len(lefts)),
        out_shape=[
            pltpu.HBM((rows, width), WIDE),
            jax.ShapeDtypeStruct((rows, 128), WIDE),
        ],
        grid=(width // wide,),
        in_specs=[whole_block(left) for left in lefts]
        + [column_block(depth, wide), column_block(1, wide)],
        out_specs=[column_block(rows, wide), pl.BlockSpec((rows, 128), lambda number: (0, 0))],
        compiler_params=pltpu.CompilerParams(**PARAMETERS),
        cost_estimate=estimate(rows, depth, width),
        name="dense_product",
    )(*lefts, weight, reward[None])


def against_dot(left, weight):
    return lax.dot_general(left, weight, (((1,), (1,)), ((), ())), preferred_element_type=WIDE)


def active_back_kernel(left_ref, weight_ref, upward_ref, to_ref):
    total = against_dot(left_ref[...], weight_ref[...])
    to_ref[...] = (total * gelu_parts(upward_ref[...])[1]).astype(LOW)


def active_back(left, weight, upward):
    (rows, depth), width, wide = left.shape, weight.shape[0], 256
    return pl.pallas_call(
        active_back_kernel,
        out_shape=jax.ShapeDtypeStruct((rows, width), LOW),
        grid=(width // wide,),
        in_specs=[
            whole_block(left),
            pl.BlockSpec((wide, depth), lambda number: (number, 0)),
            column_block(rows, wide),
        ],
        out_specs=column_block(rows, wide),
        compiler_params=pltpu.CompilerParams(**PARAMETERS),
        cost_estimate=estimate(rows, depth, width),
        name="active_back",
    )(left, weight, upward)


def against_kernel(left_ref, weight_ref, to_ref):
    to_ref[...] = against_dot(left_ref[...], weight_ref[...])


def against(left, weight):
    (rows, depth), width, wide = left.shape, weight.shape[0], 256
    return pl.pallas_call(
        against_kernel,
        out_shape=jax.ShapeDtypeStruct((rows, width), WIDE),
        grid=(width // wide,),
        in_specs=[whole_block(left), pl.BlockSpec((wide, depth), lambda number: (number, 0))],
        out_specs=column_block(rows, wide),
        compiler_params=pltpu.CompilerParams(**PARAMETERS),
        cost_estimate=estimate(rows, depth, width),
        name="against",
    )(left, weight)


def against_sums_kernel(left_ref, weight_ref, normal_ref, to_ref, sums_ref):
    total = against_dot(left_ref[...], weight_ref[...])
    to_ref[...] = total
    gain = jnp.sum(total * normal_ref[...], axis=0, keepdims=True)
    shift = jnp.sum(total, axis=0, keepdims=True)
    sums_ref[...] = jnp.concatenate([gain, shift, jnp.zeros((6, gain.shape[1]), WIDE)])


def against_sums(left, weight, normal):
    (rows, depth), width, wide = left.shape, weight.shape[0], 256
    return pl.pallas_call(
        against_sums_kernel,
        out_shape=[
            jax.ShapeDtypeStruct((rows, width), WIDE),
            jax.ShapeDtypeStruct((8, width), WIDE),
        ],
        grid=(width // wide,),
        in_specs=[
            whole_block(left),
            pl.BlockSpec((wide, depth), lambda number: (number, 0)),
            column_block(rows, wide),
        ],
        out_specs=[column_block(rows, wide), column_block(8, wide)],
        compiler_params=pltpu.CompilerParams(**PARAMETERS),
        cost_estimate=estimate(rows, depth, width),
        name="against_sums",
    )(left, weight, normal)


def rows_kernel(lefts, *refs):
    left, right = joined(refs[:lefts]), joined(refs[lefts:-1])
    total = lax.dot_general(left, right, (((0,), (0,)), ((), ())), preferred_element_type=WIDE)
    refs[-1][...] = total.astype(LOW)


def rows_product(lefts, rights):
    rows, width = lefts[0].shape[1], rights[0].shape[1]
    wide = 256
    if rows % wide:
        return inner_rows(jnp.concatenate(lefts), jnp.concatenate(rights)).astype(LOW)
    return pl.pallas_call(
        partial(rows_kernel, len(lefts)),
        out_shape=pltpu.HBM((rows, width), LOW),
        grid=(rows // wide,),
        in_specs=[pl.BlockSpec((left.shape[0], wide), lambda number: (0, number)) for left in lefts]
        + [
            pl.BlockSpec(right.shape, lambda number: (0, 0), pipeline_mode=pl.Buffered(1))
            for right in rights
        ],
        out_specs=pl.BlockSpec((wide, width), lambda number: (number, 0)),
        compiler_params=pltpu.CompilerParams(vmem_limit_bytes=16 * 2**20),
        cost_estimate=pl.CostEstimate(
            flops=4 * rows * width * sum(left.shape[0] for left in lefts),
            bytes_accessed=4 * rows * width,
            transcendentals=0,
        ),
        name="rows_product",
    )(*lefts, *rights)


def scatter_product(task, lefts, rights, rows):
    groups, me = lax.axis_size("dp"), lax.axis_index("dp")
    width = rights[0].shape[1]
    half = width // 2
    bits = list(bits_of("dp"))[1:]
    direct = rows % 128 == 0 and len(bits) == 2
    if direct:
        lefts, rights = after((lefts, rights), task.gate)
        sent = pair_product(lefts, rights, rows)
    else:
        whole = inner_rows(jnp.concatenate(after(lefts, task.gate)), jnp.concatenate(rights))
        whole = whole.astype(LOW).reshape(groups, rows, width)
        sent, kept = (
            jnp.concatenate(
                [
                    lax.dynamic_index_in_dim(whole, me ^ (2 * number + side), 0, keepdims=False)
                    for number in range(groups // 2)
                ]
            )
            for side in (1, 0)
        )
    yield [sent]
    got = swap_bit(sent, "dp", 0)
    yield [got]
    got = after(got, task.gate)
    if direct:
        table = pair_product(lefts, rights, rows, got)
        pieces = [list(table[: groups // 2]), list(table[groups // 2 :])]
    else:
        table = (kept.astype(WIDE) + got.astype(WIDE)).astype(LOW).reshape(-1, rows, width)
        pieces = [
            [table[number, :, piece * half : (piece + 1) * half] for number in range(groups // 2)]
            for piece in range(2)
        ]
    yield pieces[0] + pieces[1]
    done = [{}, {}]
    orders = [list(range(len(bits))), list(range(len(bits)))[::-1]]
    held = [list(range(groups // 2)), list(range(groups // 2))]
    late = [{}, {}]
    for step in range(len(bits)):
        soon = []
        for piece, order in enumerate(orders):
            bit = 1 << order[step]
            onward = 0 if step + 1 == len(bits) else 1 << order[step + 1]
            keep = [number for number in held[piece] if not number & bit]
            for number in keep:
                value = pieces[piece][number | bit]
                got = swap_bit(value.astype(LOW), "dp", bits[order[step]])
                if number & onward or not onward:
                    soon.append(got)
                    got = after(got, task.gate)
                    pieces[piece][number] = pieces[piece][number].astype(WIDE) + got.astype(WIDE)
                else:
                    late[piece].setdefault(number, []).append(got)
            held[piece] = keep
        yield soon
        if step + 1 < len(bits):
            yield [got for piece in range(2) for gots in late[piece].values() for got in gots]
        for piece in range(2):
            for number, gots in late[piece].items():
                for got in gots:
                    pieces[piece][number] = pieces[piece][number].astype(WIDE) + got.astype(WIDE)
            late[piece] = {}
    task.result = jnp.concatenate([pieces[0][0], pieces[1][0]], axis=1)


def scatter_groups(table):
    return lax.psum_scatter(table, "dp", scatter_dimension=0, tiled=True)


def out_product(left, right, rows):
    split, order = out_parts()
    count = left.shape[0]
    back = tuple(1 + order.index(axis) for axis in range(len(order)))
    moved = left.reshape((count,) + tuple(split[axis] for axis in order) + (rows,))
    moved = moved.transpose((0,) + back + (1 + len(split),)).reshape(count, -1)
    return inner_rows(moved, right).astype(LOW)


def rank_rows(table, rows):
    ranks, me = lax.axis_size("seq"), lax.axis_index("seq")
    return [
        lax.dynamic_slice_in_dim(table, (me + shift) % ranks * rows, rows, 0)
        for shift in range(ranks)
    ]


def swap_ranks(blocks):
    size = lax.axis_size("seq")
    return [blocks[0]] + [
        lax.ppermute(blocks[shift], "seq", [(place, (place + shift) % size) for place in range(size)])
        for shift in range(1, size)
    ]


def rows_by_rank(blocks):
    ranks, me = len(blocks), lax.axis_index("seq")
    rows = blocks[0].shape[0]
    return place_rows(
        blocks,
        [(number, 0, rows) for number in range(ranks)],
        (me + ranks - jnp.arange(ranks)) % ranks * rows,
    )


def by_number(blocks):
    return to_ring(jnp.stack(blocks))


def small_order():
    groups, ranks = lax.axis_size("dp"), lax.axis_size("seq")
    number = jnp.arange(groups * ranks)
    place = ((number // ranks) ^ lax.axis_index("dp")) * ranks + (
        (number % ranks) ^ lax.axis_index("seq")
    )
    return (place[:, None] == number[None, :]).astype(WIDE)


def scatter_small(table, done):
    table = jnp.dot(
        small_order().T, table, precision=lax.Precision.HIGHEST, preferred_element_type=WIDE
    )
    for axis in ("dp", "seq"):
        for bit in reversed(bits_of(axis)):
            half = table.shape[0] // 2
            table = table[:half] + swap_bit(table[half:], axis, bit)
        table = after(table, done)
    return table[0]


def sum_ranks(table):
    size = lax.axis_size("seq")
    total = table
    for shift in range(1, size):
        total = total + lax.ppermute(
            table, "seq", [(place, (place + shift) % size) for place in range(size)]
        )
    return total


def spread_path(
    inputs,
    cotangent,
    segments,
    labels,
    step_ends,
    attend_gain,
    attend_shift,
    project_in,
    project_bias,
    project_out,
    output_bias,
    dense_gain,
    dense_shift,
    up_weight,
    up_bias,
    down_weight,
    down_bias,
    reward_weight,
):
    groups, ranks = lax.axis_size("dp"), lax.axis_size("seq")
    rank = lax.axis_index("seq")
    rows_here, places_here, width = inputs.shape
    all_rows = rows_here * groups
    head_width = width // HEADS
    heads_here = HEADS // ranks
    share = heads_here * head_width
    rows_in = project_in.shape[0]
    hidden_here = down_weight.shape[0]
    length = ranks * places_here
    score_scale = head_width ** (-0.5)

    small = (
        attend_gain,
        attend_shift,
        project_bias,
        output_bias,
        dense_gain,
        dense_shift,
        up_bias,
        down_bias,
        reward_weight,
    )
    sizes = [vector.shape[0] for vector in small]
    riders = [vector.reshape(-(-vector.shape[0] // 128), -1) for vector in small]
    riders += [segments, labels, step_ends]
    out_moved = lax.ppermute(project_out, EVERY, out_route())
    weight_out = out_gather(out_moved)
    dealt_in = deal(project_in, head_pieces, head_width, riders)
    came_in = swap_ranks(dealt_in)
    rows_in_all = rows_by_rank(came_in)
    gathered = gather_groups(rows_in_all)
    inputs_ring = ring_gather(
        after(inputs[0], came_in), [idle, lambda gate: [weight_out], idle]
    )
    dealt_up = deal(after(up_weight, [rows_in_all]), hidden_pieces, hidden_here)
    came_up = swap_ranks(after(dealt_up, [inputs_ring[-1]]))
    riders = gathered[:, 3 * share :]
    riders = riders.reshape(groups * ranks, rows_in, 128).astype(WIDE)
    vectors = []
    row = 0
    for size in sizes + [places_here] * 3:
        lines = -(-size // 128)
        vectors.append(
            riders[:, row : row + lines].reshape(groups * ranks, -1)[:, :size].reshape(-1)
        )
        row += lines
    gain_one, shift_one, bias_in, bias_out, gain_two, shift_two, bias_up, bias_down, reward_wide = (
        vectors[: len(sizes)]
    )

    held = own_heads()
    bias_heads = exact(held, bias_in.reshape(2, HEADS, head_width).transpose(1, 0, 2).reshape(HEADS, -1))
    bias_heads = bias_heads.reshape(heads_here, 2, head_width)
    bias_full = jnp.concatenate(
        [bias_heads[:, 0].reshape(-1), jnp.zeros((share,), WIDE), bias_heads[:, 1].reshape(-1)]
    )
    bias_up_here = lax.dynamic_index_in_dim(
        bias_up.reshape(groups, ranks, hidden_here), rank, 1, keepdims=False
    ).reshape(-1)
    marks = jnp.stack(
        [
            lax.dynamic_index_in_dim(
                mark.reshape(groups, ranks, places_here), lax.axis_index("dp"), 0, keepdims=False
            )
            for mark in vectors[len(sizes) :]
        ],
        axis=1,
    )
    marks_ring = to_ring(marks)
    segments_ring = marks_ring[:, 0].reshape(-1)
    places_ring = to_ring(jnp.arange(length).reshape(ranks, places_here)).reshape(-1)

    own = inputs[0].astype(WIDE)
    firsts, first_normals = [], []
    for block in inputs_ring:
        value, normal, inverse = normalize_parts(block.astype(WIDE), gain_one, shift_one)
        if not firsts:
            first_inverse = inverse
        firsts.append(value.astype(LOW))
        first_normals.append(normal)
    first_low = jnp.concatenate(firsts)
    projected = project(first_low, gathered, bias_full)
    came_up, projected = lax.optimization_barrier((came_up, projected))
    rows_up_all = rows_by_rank(came_up)
    weight_up = gather_groups(rows_up_all)
    weight_down = gather_groups(after(down_weight, [rows_up_all]))

    def heads(block):
        return block.reshape(length, heads_here, head_width)

    queries, keys, values = (
        heads(projected[:, :share]),
        heads(projected[:, share : 2 * share]),
        heads(projected[:, 2 * share :]),
    )
    same = (segments_ring[None, :] == 0) | (segments_ring[None, :] == segments_ring[:, None])
    allowed = same & (places_ring[None, :] <= places_ring[:, None])
    scores = jnp.einsum("qhd,khd->hqk", queries, keys, preferred_element_type=WIDE) * score_scale
    scores = jnp.where(allowed[None], scores, MASKED)
    highest = jnp.max(scores, axis=-1, keepdims=True)
    exponent = jnp.exp(scores - highest)
    totals = jnp.sum(exponent, axis=-1, keepdims=True)
    chances = exponent / totals
    chances_low = chances.astype(LOW)
    mixture = jnp.einsum("hqk,khd->qhd", chances_low, values, preferred_element_type=WIDE)
    mixture = mixture.reshape(length, share).astype(LOW)

    def block_of(array, k):
        return array[k * places_here : (k + 1) * places_here]

    mixture_late = mixture
    branch = ring_sum(lambda k, gate: product(block_of(mixture, k), weight_out))
    hidden = own + branch + bias_out

    second_value, second_normal, second_inverse = normalize_parts(hidden, gain_two, shift_two)

    seconds, found = ring_gather(
        second_value.astype(LOW),
        use=lambda k, block: upward_product(block, weight_up, bias_up_here),
        plan=(1, 1, 1),
    )
    upwards, activated = map(list, zip(*found))
    cotangent_task = Task(ring_gather_task, after(cotangent[0], [seconds[-1]]))
    activated[-1] = after(activated[-1], cotangent_task.go())
    dense_all, reward_lanes = dense_product(activated, weight_down, reward_wide)
    dense_parts = [block_of(dense_all, k) for k in range(ranks)]
    reward_lanes = after(reward_lanes, cotangent_task.go())
    reward_parts = list(jnp.sum(reward_lanes, axis=-1).reshape(ranks, places_here))
    result_task = Task(ring_sum_task, dense_parts)

    reward_parts[0] = reward_parts[0] + jnp.sum((hidden + bias_down) * reward_wide, axis=-1)
    rewards_all = sum_ranks(to_ring(jnp.stack(reward_parts)))
    scored = marks[:, 2] * (marks[:, 0] > 0)
    error_all = scored * (jax.nn.sigmoid(rewards_all) - marks[:, 1]) / all_rows
    error_ring = to_ring(error_all)
    rewards = lax.dynamic_index_in_dim(rewards_all, rank, 0, keepdims=False)

    result_grads, dense_lows, upward_lows = [], [], [None] * ranks

    def dense_grad():
        k = len(result_grads)
        block = cotangent_task.result[k].astype(WIDE)
        result_grads.append(block + error_ring[k][:, None] * reward_wide)
        dense_lows.append(result_grads[-1].astype(LOW))

    def second_part(k, gate):
        while len(dense_lows) <= k:
            dense_grad()
        upward_lows[k] = active_back(after(dense_lows[k], gate), weight_down, upwards[k])
        return against(upward_lows[k], weight_up)

    reward_weight_gradient = jnp.sum(error_ring.reshape(-1)[:, None] * dense_all, axis=0)
    reward_weight_gradient += jnp.sum(error_ring[0][:, None] * (hidden + bias_down), axis=0)
    error_ring = after(error_ring, cotangent_task.go())
    down_table = None

    def down_start(gate):
        nonlocal down_table
        down_table = rows_product(after(activated, gate), dense_lows)
        return [down_table]

    second_grad = ring_sum(second_part, [idle, down_start, idle])
    down_weight_gradient = scatter_groups(down_table).astype(WIDE)
    result_grad = result_grads[0]
    down_bias_gradient = jnp.sum(dense_lows[0].astype(WIDE), axis=0)
    upward_all = jnp.concatenate(upward_lows)
    up_bias_gradient = jnp.sum(upward_all.astype(WIDE), axis=0)
    dense_gain_gradient = jnp.sum(second_grad * second_normal, axis=0)
    dense_shift_gradient = jnp.sum(second_grad, axis=0)
    hidden_grad = result_grad + normalize_back(second_grad, second_normal, second_inverse, gain_two)

    branch_low = hidden_grad.astype(LOW)
    up_task = Task(scatter_product, seconds, upward_lows, ranks * rows_in)
    branch_low = after(branch_low, up_task.go())
    output_bias_gradient = jnp.sum(branch_low.astype(WIDE), axis=0)
    up_bias_gradient = lax.dynamic_update_index_in_dim(
        jnp.zeros((groups, ranks, hidden_here), WIDE),
        up_bias_gradient.reshape(groups, hidden_here),
        rank,
        1,
    )

    def by_device(vectors):
        return jnp.concatenate([vector.reshape(groups * ranks, -1) for vector in vectors], axis=1)

    early = by_device(
        (
            output_bias_gradient,
            dense_gain_gradient,
            dense_shift_gradient,
            up_bias_gradient,
            down_bias_gradient,
            reward_weight_gradient,
        )
    )
    branch_lows = ring_gather(
        branch_low,
        [up_task.go, lambda gate: up_task.go(gate) + [early], up_task.go],
    )
    branch_lows[-1], early = lax.optimization_barrier((branch_lows[-1], early))
    branch_all = jnp.concatenate(branch_lows)
    mixture_grad = against_rows(branch_all, weight_out).astype(LOW)
    out_table = out_product(mixture_late, branch_all, project_out.shape[0])
    out_summed = scatter_groups(out_table)
    grad_heads = heads(mixture_grad)
    chance_grad = jnp.einsum("qhd,khd->hqk", grad_heads, values, preferred_element_type=WIDE)
    weighted = jnp.sum(chances * chance_grad, axis=-1, keepdims=True)
    score_grad = (chances * (chance_grad - weighted)).astype(LOW)
    score_grad = after(score_grad, result_task.go([mixture_grad]))
    query_grad = jnp.einsum("hqk,khd->qhd", score_grad, keys, preferred_element_type=WIDE)
    key_grad = jnp.einsum("hqk,qhd->khd", score_grad, queries, preferred_element_type=WIDE)
    value_grad = jnp.einsum("hqk,qhd->khd", chances_low, grad_heads, preferred_element_type=WIDE)
    projected_grad = jnp.concatenate(
        [
            (query_grad * score_scale).reshape(length, share).astype(LOW),
            (key_grad * score_scale).reshape(length, share).astype(LOW),
            value_grad.reshape(length, share).astype(LOW),
        ],
        axis=1,
    )
    in_task = Task(scatter_product, firsts, [projected_grad], ranks * rows_in)
    projected_grad = after(projected_grad, in_task.go() + result_task.go([score_grad]))
    first_sums = [None] * ranks

    def first_part(k, gate):
        block = after(block_of(projected_grad, k), gate)
        term, first_sums[k] = against_sums(block, gathered, first_normals[k])
        return term

    first_grad = ring_sum(
        first_part,
        [
            lambda gate: in_task.go(gate) + up_task.go(gate),
            lambda gate: in_task.go(gate) + up_task.go(gate),
            in_task.go,
        ],
    )
    came_up = swap_ranks(rank_rows(after(up_task.finish().astype(LOW), [first_grad]), rows_in))
    in_task.go([first_grad])
    in_task.go([first_grad])
    result_task.go([first_grad])
    result = hidden + result_task.finish() + bias_down
    result_low = result.astype(LOW)
    project_out_gradient = lax.ppermute(
        out_summed, EVERY, [(there, here) for here, there in out_route()]
    ).astype(WIDE)
    up_weight_gradient = collect(came_up, hidden_pieces, hidden_here)
    bias_sums = jnp.sum(projected_grad.astype(WIDE), axis=0)

    bias_heads = jnp.concatenate([bias_sums[:share], bias_sums[2 * share :]])
    bias_heads = bias_heads.reshape(2, heads_here, head_width)
    project_bias_gradient = jnp.concatenate(
        [exact(held.T, bias_heads[which]).reshape(-1) for which in range(2)]
    )
    attend_gain_gradient, attend_shift_gradient = sum(first_sums)[:2]
    inputs_gradient = hidden_grad + normalize_back(
        first_grad, first_normals[0], first_inverse, gain_one
    )
    late = by_device((attend_gain_gradient, attend_shift_gradient, project_bias_gradient))
    table = jnp.concatenate([late, early], axis=1)
    summed = scatter_small(table, came_up)
    in_summed = after(in_task.finish().astype(LOW), [summed] + came_up)
    came_in = swap_ranks(rank_rows(in_summed, rows_in))
    project_in_gradient = collect(came_in, head_pieces, head_width)
    parts = []
    start = 0
    for size in sizes:
        parts.append(summed[start : start + size])
        start += size
    return (
        result_low[None],
        rewards[None],
        inputs_gradient[None],
        parts[0],
        parts[1],
        project_in_gradient,
        parts[2],
        project_out_gradient,
        parts[3],
        parts[4],
        parts[5],
        up_weight_gradient,
        parts[6],
        down_weight_gradient,
        parts[7],
        parts[8],
    )


def solution(mesh):
    row = P("dp", "seq")
    wide_row = P("dp", "seq", None)
    vector = P(("dp", "seq"))
    matrix = P(("dp", "seq"), None)
    in_specs = (
        wide_row,
        wide_row,
        row,
        row,
        row,
        vector,
        vector,
        matrix,
        vector,
        matrix,
        vector,
        vector,
        vector,
        matrix,
        vector,
        matrix,
        vector,
        vector,
    )
    out_specs = (
        wide_row,
        row,
        wide_row,
        vector,
        vector,
        matrix,
        vector,
        matrix,
        vector,
        vector,
        vector,
        matrix,
        vector,
        matrix,
        vector,
        vector,
    )
    return jax.shard_map(
        spread_path, mesh=mesh, in_specs=in_specs, out_specs=out_specs, check_vma=False
    )
```

time: 870 us -> 593 us (0.68)
  waiting for transfers between devices: 519 us -> 218 us
  blocking collectives: 124 us -> 0 us
  Pallas kernels: 0 us -> 122 us
  matrix products: 123 us -> 21.7 us
  starting transfers between devices: 21.7 us -> 85.2 us
  local copies, waits for them, and re-layouts: 34.4 us -> 74.1 us
  other arithmetic: 23.6 us -> 45 us
    reduce_scatter x4 -> x2, waiting for transfers between devices: 162 us -> 0.01 us  [scatter_groups(): return lax.psum_scatter(table, 'dp', scatter_dimension=0, tiled=True)]
    pallas_call x0 -> x29, Pallas kernels: none -> 122 us  [the longest x4 22.7 us: pair_product(): pl.pallas_call(partial(pair_kernel, len(lefts), len(rights), kept), out_s...]
    unnamed x10 -> x6, waiting for transfers between devices: 121 us -> 0.61 us
    ppermute x26 -> x60, starting transfers between devices: 12.4 us -> 85 us  [the longest x12 33.5 us: swap_ranks(): lax.ppermute(blocks[shift], 'seq', [(place, (place + shift) % size) for p...]
    all_to_all x2 -> x0, blocking collectives: 62.8 us -> none  [swap_ranks(): lax.all_to_all(blocks, 'seq', split_axis=0, concat_axis=0, tiled=True)]
    dot_general x16 -> x1, matrix products: 52.1 us -> 2.96 us  [against_rows(): return jnp.einsum('tb,ab->ta', left, right, preferred_element_type=WIDE)]
    unnamed x197 -> x244, local copies, waits for them, and re-layouts: 10.4 us -> 51.5 us
    unnamed x1 -> x0, blocking collectives: 39.9 us -> none
  transfers between devices with their start and end apart: 37 -> 66, of which waited for: 26 -> 34; matrix products, arithmetic and copies ran while one was open for 16% -> 14% of each run, Pallas kernels for 0% -> 18%
where the time goes in v2:
time: 593 us; the launch traced here: 582 us
  waiting for transfers between devices  218 us (37%)
  Pallas kernels  122 us (21%)
  starting transfers between devices  85.2 us (14%)
  local copies, waits for them, and re-layouts  74.1 us (12%)
  other arithmetic  45 us (8%)
  matrix products  21.7 us (4%)
  between operations  16.4 us (3%)
    ppermute x9, waiting for transfers between devices, ring_sum(): moved = lax.ppermute(sent, 'seq', ring_next())  76.5 us
    ppermute x9, waiting for transfers between devices, ring_gather(): moved = lax.ppermute(block, 'seq', ring_next())  66.4 us
    unnamed x244, local copies, waits for them, and re-layouts  51.5 us
    ppermute x12, starting transfers between devices, swap_ranks(): lax.ppermute(blocks[shift], 'seq', [(place, (place + shift) % size) for p...  33.5 us
    ppermute x12, waiting for transfers between devices, swap_ranks(): lax.ppermute(blocks[shift], 'seq', [(place, (place + shift) % size) for p...  27 us
    ppermute x19, starting transfers between devices, swap_bit(): lax.ppermute(block, axis, [(place, place ^ 1 << bit) for place in range(l...  26.1 us
    pallas_call x4, Pallas kernels, pair_product(): pl.pallas_call(partial(pair_kernel, len(lefts), len(rights), kept), out_s...  22.7 us
    pallas_call x4, Pallas kernels, active_back(): pl.pallas_call(active_back_kernel, out_shape=jax.ShapeDtypeStruct((rows,...  16.3 us
  transfers between devices with their start and end apart: 66, of which 34 were waited for; matrix products, arithmetic and copies ran while one was open for 14% of the time, Pallas kernels for 18%

profile of v2, /device:TPU:0, one launch (start us, length us, event | category | flops | bytes accessed | tf_op | source)
XLA Modules:
  0.0 582.2 jit_solution(996203732628254473)
XLA Ops:
  12.0 12.5 %collective-permute-start = (bf16[64,1664]{1,0:T(8,128)(2,1)}, bf16[64,1664]{1,0:T(8,128)(2,1)S(1)}, u32[]{:S(2)}, u32[]{:S(2)}) collective-permute-start(bf16[64,1664]{1,0:T(8,128)(2,1)} %get-tuple-element.136), channel_id=1, source_target_pairs={{0,1},{1,2},{2,3},{3,0},{4,5},{5,6},{6,7},{7,4},{8,9},{9,10},{10,1... | collective-permute-start | bytes 638984 | tf_op jit(solution)/shard_map/ppermute | solution.py:719
  27.1 5.9 %collective-permute-done.refs_1_ = bf16[64,1664]{1,0:T(8,128)(2,1)S(1)} collective-permute-done((bf16[64,1664]{1,0:T(8,128)(2,1)}, bf16[64,1664]{1,0:T(8,128)(2,1)S(1)}, u32[]{:S(2)}, u32[]{:S(2)}) %collective-permute-start) | collective-permute-done | bytes 213024 | tf_op jit(solution)/shard_map/ppermute | solution.py:719
  33.0 7.3 %collective-permute-done.1.refs_2_ = bf16[64,1664]{1,0:T(8,128)(2,1)S(1)} collective-permute-done((bf16[64,1664]{1,0:T(8,128)(2,1)}, bf16[64,1664]{1,0:T(8,128)(2,1)S(1)}, u32[]{:S(2)}, u32[]{:S(2)}) %collective-permute-start.1) | collective-permute-done | bytes 213024 | tf_op jit(solution)/shard_map/ppermute | solution.py:719
  44.7 5.0 collective-permute-start.3
  52.5 8.7 %collective-permute-done.3 = bf16[128,2048]{1,0:T(8,128)(2,1)S(1)} collective-permute-done((bf16[128,2048]{1,0:T(8,128)(2,1)S(1)}, bf16[128,2048]{1,0:T(8,128)(2,1)S(1)}, u32[]{:S(2)}, u32[]{:S(2)}) %collective-permute-start.3) | collective-permute-done | bytes 524320 | tf_op jit(solution)/shard_map/ppermute | solution.py:77
  64.2 3.2 copy.69
  67.4 8.8 %collective-permute-done.4 = bf16[128,2048]{1,0:T(8,128)(2,1)S(1)} collective-permute-done((bf16[128,2048]{1,0:T(8,128)(2,1)S(1)}, bf16[128,2048]{1,0:T(8,128)(2,1)S(1)}, u32[]{:S(2)}, u32[]{:S(2)}) %collective-permute-start.4) | collective-permute-done | bytes 524320 | tf_op jit(solution)/shard_map/ppermute | solution.py:77
  77.3 12.9 %collective-permute-done.6 = bf16[128,2048]{1,0:T(8,128)(2,1)S(1)} collective-permute-done((bf16[128,2048]{1,0:T(8,128)(2,1)S(1)}, bf16[128,2048]{1,0:T(8,128)(2,1)S(1)}, u32[]{:S(2)}, u32[]{:S(2)}) %collective-permute-start.6) | collective-permute-done | bytes 524320 | tf_op jit(solution)/shard_map/ppermute | solution.py:77
  90.2 3.7 collective-permute-start.9
  94.4 4.8 all-gather.6.cloned.1.call-done.weight_ref
  107.9 5.0 project.1
  119.7 3.7 fusion.81
  129.4 13.8 %collective-permute-done.10 = bf16[128,2048]{1,0:T(8,128)(2,1)S(1)} collective-permute-done((bf16[128,2048]{1,0:T(8,128)(2,1)S(1)}, bf16[128,2048]{1,0:T(8,128)(2,1)S(1)}, u32[]{:S(2)}, u32[]{:S(2)}) %collective-permute-start.10) | collective-permute-done | bytes 524320 | tf_op jit(solution)/shard_map/ppermute | solution.py:97
  143.8 14.6 %collective-permute-done.11 = bf16[128,2048]{1,0:T(8,128)(2,1)S(1)} collective-permute-done((bf16[128,2048]{1,0:T(8,128)(2,1)S(1)}, bf16[128,2048]{1,0:T(8,128)(2,1)S(1)}, u32[]{:S(2)}, u32[]{:S(2)}) %collective-permute-start.11) | collective-permute-done | bytes 524320 | tf_op jit(solution)/shard_map/ppermute | solution.py:97
  160.4 13.6 %collective-permute-done.12 = bf16[128,2048]{1,0:T(8,128)(2,1)S(1)} collective-permute-done((bf16[128,2048]{1,0:T(8,128)(2,1)}, bf16[128,2048]{1,0:T(8,128)(2,1)S(1)}, u32[]{:S(2)}, u32[]{:S(2)}) %collective-permute-start.12) | collective-permute-done | bytes 524320 | tf_op jit(solution)/shard_map/ppermute | solution.py:97
  176.5 4.2 copy-done
  180.7 4.1 upward_product.4
  185.6 3.2 collective-permute-done.13.left_ref.refs_1_
  188.8 4.1 upward_product.5
  192.9 8.2 %collective-permute-done.14.left_ref.refs_2_ = bf16[128,2048]{1,0:T(8,128)(2,1)S(1)} collective-permute-done((bf16[128,2048]{1,0:T(8,128)(2,1)S(1)}, bf16[128,2048]{1,0:T(8,128)(2,1)S(1)}, u32[]{:S(2)}, u32[]{:S(2)}) %collective-permute-start.14) | collective-permute-done | bytes 524320 | tf_op jit(solution)/shard_map/ppermute | solution.py:77
  201.2 4.1 upward_product.6
  207.0 6.0 %collective-permute-done.15.left_ref.refs_3_ = bf16[128,2048]{1,0:T(8,128)(2,1)S(1)} collective-permute-done((bf16[128,2048]{1,0:T(8,128)(2,1)S(1)}, bf16[128,2048]{1,0:T(8,128)(2,1)S(1)}, u32[]{:S(2)}, u32[]{:S(2)}) %collective-permute-start.15) | collective-permute-done | bytes 524320 | tf_op jit(solution)/shard_map/ppermute | solution.py:77
  213.1 3.5 copy-done.2
  216.6 4.1 upward_product.7
  221.5 4.2 collective-permute-done.16
  225.8 3.4 copy-done.4
  233.3 8.0 %dense_product.1 = (f32[512,2048]{1,0:T(8,128)}, f32[512,128]{1,0:T(8,128)S(1)}) custom-call(bf16[128,2048]{1,0:T(8,128)(2,1)S(1)} %copy-done.47, bf16[128,2048]{1,0:T(8,128)(2,1)S(1)} %copy-done.50, bf16[128,2048]{1,0:T(8,128)(2,1)S(1)} %copy-done.53, bf16[128,2048]{1,0:T(8,128)(2,1)S(1)} %copy-done.56, bf16[2048,2048]{1,0:T(8,128)(2,1)S(1)} %copy-done.4, ...), custom_call_target="tpu_custom_call" | custom-call | flops 8589934592 | bytes 8388608 | tf_op jit(solution)/shard_map/dense_product/pallas_call | solution.py:508
  249.0 8.4 %collective-permute-done.19 = f32[4,128]{1,0:T(4,128)S(1)} collective-permute-done((f32[4,128]{1,0:T(4,128)S(1)}, f32[4,128]{1,0:T(4,128)S(1)}, u32[]{:S(2)}, u32[]{:S(2)}) %collective-permute-start.19) | collective-permute-done | bytes 2080 | tf_op jit(solution)/shard_map/ppermute | solution.py:763
  260.2 3.6 copy-done.5
  263.7 4.1 active_back.4.left_ref.refs_5_
  267.8 3.4 copy-done.3
  271.2 4.0 against.4
  275.9 4.1 active_back.5.left_ref.refs_6_
  280.0 4.0 against.5
  284.1 5.8 collective-permute-done.23
  290.8 4.1 active_back.6.left_ref.refs_7_
  294.9 4.0 against.6
  299.0 8.0 %rows_product.1 = bf16[2048,2048]{1,0:T(8,128)(2,1)} custom-call(bf16[128,2048]{1,0:T(8,128)(2,1)S(1)} %copy-done.48, bf16[128,2048]{1,0:T(8,128)(2,1)S(1)} %copy-done.51, bf16[128,2048]{1,0:T(8,128)(2,1)S(1)} %copy-done.54, bf16[128,2048]{1,0:T(8,128)(2,1)S(1)} %copy-done.57, bf16[128,2048]{1,0:T(8,128)(2,1)S(1)} %get-tuple-element.184.refs_4_.left_ref, ...), custom_call_target="tpu_custom_call" | custom-call | flops 8589934592 | bytes 16777216 | tf_op jit(solution)/shard_map/rows_product/pallas_call | solution.py:609
  308.5 3.4 copy-done.7
  311.9 4.1 active_back.7.left_ref.refs_4_
  316.0 4.6 pair_product.4
  320.7 4.0 against.7
  324.7 12.4 %collective-permute-done.25 = bf16[128,2048]{1,0:T(8,128)(2,1)S(1)} collective-permute-done((bf16[128,2048]{1,0:T(8,128)(2,1)S(1)}, bf16[128,2048]{1,0:T(8,128)(2,1)S(1)}, u32[]{:S(2)}, u32[]{:S(2)}) %collective-permute-start.25) | collective-permute-done | bytes 524320 | tf_op jit(solution)/shard_map/ppermute | solution.py:97
  342.8 14.0 %collective-permute-done.26 = bf16[128,2048]{1,0:T(8,128)(2,1)} collective-permute-done((bf16[128,2048]{1,0:T(8,128)(2,1)}, bf16[128,2048]{1,0:T(8,128)(2,1)}, u32[]{:S(2)}, u32[]{:S(2)}) %collective-permute-start.26) | collective-permute-done | bytes 524320 | tf_op jit(solution)/shard_map/ppermute | solution.py:77
  361.0 7.4 %pair_product.5 = (bf16[256,1024]{1,0:T(8,128)(2,1)}, bf16[256,1024]{1,0:T(8,128)(2,1)}, bf16[256,1024]{1,0:T(8,128)(2,1)}, bf16[256,1024]{1,0:T(8,128)(2,1)}, b...) custom-call(s32[1]{0:T(128)} %bitcast.53.me_ref, ...), custom_call_target="tpu_custom_call" | custom-call | flops 4294967296 | bytes 8388608 | tf_op jit(solution)/shard_map/pair_product/pallas_call | solution.py:396
  375.2 6.4 %collective-permute-done.30 = bf16[256,1024]{1,0:T(8,128)(2,1)} collective-permute-done((bf16[256,1024]{1,0:T(8,128)(2,1)}, bf16[256,1024]{1,0:T(8,128)(2,1)}, u32[]{:S(2)}, u32[]{:S(2)}) %collective-permute-start.30) | collective-permute-done | bytes 524320 | tf_op jit(solution)/shard_map/ppermute | solution.py:347
  399.5 4.8 collective-permute-done.17
  407.5 3.3 convolution_convert_fusion.3
  413.5 3.9 pair_product.6
  426.1 11.2 %collective-permute-done.32 = bf16[128,2048]{1,0:T(8,128)(2,1)S(1)} collective-permute-done((bf16[128,2048]{1,0:T(8,128)(2,1)S(1)}, bf16[128,2048]{1,0:T(8,128)(2,1)S(1)}, u32[]{:S(2)}, u32[]{:S(2)}) %collective-permute-start.32) | collective-permute-done | bytes 524320 | tf_op jit(solution)/shard_map/ppermute | solution.py:114
  440.2 3.3 copy-done.8
  443.5 3.8 against_sums.4
  452.2 3.8 against_sums.5
  456.4 7.7 %collective-permute-done.34 = bf16[128,2048]{1,0:T(8,128)(2,1)S(1)} collective-permute-done((bf16[128,2048]{1,0:T(8,128)(2,1)S(1)}, bf16[128,2048]{1,0:T(8,128)(2,1)S(1)}, u32[]{:S(2)}, u32[]{:S(2)}) %collective-permute-start.34) | collective-permute-done | bytes 524320 | tf_op jit(solution)/shard_map/ppermute | solution.py:97
  466.4 6.9 %pair_product.7 = (bf16[256,768]{1,0:T(8,128)(2,1)}, bf16[256,768]{1,0:T(8,128)(2,1)}, bf16[256,768]{1,0:T(8,128)(2,1)}, bf16[256,768]{1,0:T(8,128)(2,1)}, bf16[...) custom-call(s32[1]{0:T(128)} %bitcast.53.me_ref, ...), custom_call_target="tpu_custom_call" | custom-call | flops 3221225472 | bytes 6291456 | tf_op jit(solution)/shard_map/pair_product/pallas_call | solution.py:396
  475.6 3.6 collective-permute-start.59
  483.2 3.8 against_sums.6
  489.9 3.8 against_sums.7
  507.1 8.6 %collective-permute-done.41 = bf16[128,2048]{1,0:T(8,128)(2,1)S(1)} collective-permute-done((bf16[128,2048]{1,0:T(8,128)(2,1)S(1)}, bf16[128,2048]{1,0:T(8,128)(2,1)S(1)}, u32[]{:S(2)}, u32[]{:S(2)}) %collective-permute-start.41) | collective-permute-done | bytes 524320 | tf_op jit(solution)/shard_map/ppermute | solution.py:97
  524.2 5.6 collective-permute-start.48
  533.9 8.2 %collective-permute-done.48.refs_2_ = bf16[64,2048]{1,0:T(8,128)(2,1)S(1)} collective-permute-done((bf16[64,2048]{1,0:T(8,128)(2,1)S(1)}, bf16[64,2048]{1,0:T(8,128)(2,1)S(1)}, u32[]{:S(2)}, u32[]{:S(2)}) %collective-permute-start.48) | collective-permute-done | bytes 262176 | tf_op jit(solution)/shard_map/ppermute | solution.py:719
  542.4 4.3 collective-permute-start.50
  548.3 4.2 collective-permute-start.51
  563.6 5.3 collective-permute-done.57.refs_2_
  (511 shorter events, 179.6 us)
Async XLA Ops:
  7.2 56.9 %all-gather.12.cloned.1.call-start = ((), (), s32[]{:S(2)}) async-start(), calls=%async_computation.7 | async-start | bytes 2359296 | tf_op jit(solution)/shard_map/all_gather | solution.py:336
  9.7 89.5 %all-gather.6.cloned.1.call-start = ((), (), s32[]{:S(2)}) async-start(), calls=%async_computation.2 | async-start | bytes 7667712 | tf_op jit(solution)/shard_map/all_gather | solution.py:343
  12.0 21.0 %collective-permute-start = (bf16[64,1664]{1,0:T(8,128)(2,1)}, bf16[64,1664]{1,0:T(8,128)(2,1)S(1)}, u32[]{:S(2)}, u32[]{:S(2)}) collective-permute-start(bf16[64,1664]{1,0:T(8,128)(2,1)} %get-tuple-element.136), channel_id=1, source_target_pairs={{0,1},{1,2},{2,3},{3,0},{4,5},{5,6},{6,7},{7,4},{8,9},{9,10},{10,1... | collective-permute-start | bytes 638984 | tf_op jit(solution)/shard_map/ppermute | solution.py:719
  24.5 15.8 %collective-permute-start.1 = (bf16[64,1664]{1,0:T(8,128)(2,1)}, bf16[64,1664]{1,0:T(8,128)(2,1)S(1)}, u32[]{:S(2)}, u32[]{:S(2)}) collective-permute-start(bf16[64,1664]{1,0:T(8,128)(2,1)} %get-tuple-element.137), channel_id=1, source_target_pairs={{0,2},{1,3},{2,0},{3,1},{4,6},{5,7},{6,4},{7,5},{8,10},{9,11},{10,... | collective-permute-start | bytes 638984 | tf_op jit(solution)/shard_map/ppermute | solution.py:719
  27.1 13.2 %collective-permute-start.2 = (bf16[64,1664]{1,0:T(8,128)(2,1)}, bf16[64,1664]{1,0:T(8,128)(2,1)S(1)}, u32[]{:S(2)}, u32[]{:S(2)}) collective-permute-start(bf16[64,1664]{1,0:T(8,128)(2,1)} %get-tuple-element.138), channel_id=1, source_target_pairs={{0,3},{1,0},{2,1},{3,2},{4,7},{5,4},{6,5},{7,6},{8,11},{9,8},{10,9... | collective-permute-start | bytes 638984 | tf_op jit(solution)/shard_map/ppermute | solution.py:719
  43.9 132.6 %all-gather.8.cloned.1.call-start = ((), (), s32[]{:S(2)}) async-start(), calls=%async_computation.3 | async-start | bytes 9437184 | tf_op jit(solution)/shard_map/all_gather | solution.py:343
  44.7 16.5 %collective-permute-start.3 = (bf16[128,2048]{1,0:T(8,128)(2,1)S(1)}, bf16[128,2048]{1,0:T(8,128)(2,1)S(1)}, u32[]{:S(2)}, u32[]{:S(2)}) collective-permute-start(bf16[128,2048]{1,0:T(8,128)(2,1)S(1)} %bitcast.195), channel_id=1, source_target_pairs={{0,1},{1,2},{2,3},{3,0},{4,5},{5,6},{6,7},{7,4},{8,9},{9,10},{10,1... | collective-permute-start | bytes 1572872 | tf_op jit(solution)/shard_map/ppermute | solution.py:77
  61.2 14.9 %collective-permute-start.4 = (bf16[128,2048]{1,0:T(8,128)(2,1)S(1)}, bf16[128,2048]{1,0:T(8,128)(2,1)S(1)}, u32[]{:S(2)}, u32[]{:S(2)}) collective-permute-start(bf16[128,2048]{1,0:T(8,128)(2,1)S(1)} %collective-permute-done.3), channel_id=1, source_target_pairs={{0,1},{1,2},{2,3},{3,0},{4,5},{5,6},{6,7},{7,4},{8,9},{9,10},{10,1... | collective-permute-start | bytes 1572872 | tf_op jit(solution)/shard_map/ppermute | solution.py:77
  76.1 14.0 %collective-permute-start.6 = (bf16[128,2048]{1,0:T(8,128)(2,1)S(1)}, bf16[128,2048]{1,0:T(8,128)(2,1)S(1)}, u32[]{:S(2)}, u32[]{:S(2)}) collective-permute-start(bf16[128,2048]{1,0:T(8,128)(2,1)S(1)} %collective-permute-done.4), channel_id=1, source_target_pairs={{0,1},{1,2},{2,3},{3,0},{4,5},{5,6},{6,7},{7,4},{8,9},{9,10},{10,1... | collective-permute-start | bytes 1572872 | tf_op jit(solution)/shard_map/ppermute | solution.py:77
  90.1 22.8 %collective-permute-start.7 = (bf16[64,2048]{1,0:T(8,128)(2,1)}, bf16[64,2048]{1,0:T(8,128)(2,1)S(1)}, u32[]{:S(2)}, u32[]{:S(2)}) collective-permute-start(bf16[64,2048]{1,0:T(8,128)(2,1)} %get-tuple-element.147), channel_id=1, source_target_pairs={{0,1},{1,2},{2,3},{3,0},{4,5},{5,6},{6,7},{7,4},{8,9},{9,10},{10,1... | collective-permute-start | bytes 786440 | tf_op jit(solution)/shard_map/ppermute | solution.py:719
  90.1 22.8 %collective-permute-start.8 = (bf16[64,2048]{1,0:T(8,128)(2,1)}, bf16[64,2048]{1,0:T(8,128)(2,1)S(1)}, u32[]{:S(2)}, u32[]{:S(2)}) collective-permute-start(bf16[64,2048]{1,0:T(8,128)(2,1)} %get-tuple-element.148), channel_id=1, source_target_pairs={{0,2},{1,3},{2,0},{3,1},{4,6},{5,7},{6,4},{7,5},{8,10},{9,11},{10,... | collective-permute-start | bytes 786440 | tf_op jit(solution)/shard_map/ppermute | solution.py:719
  90.2 22.7 %collective-permute-start.9 = (bf16[64,2048]{1,0:T(8,128)(2,1)S(1)}, bf16[64,2048]{1,0:T(8,128)(2,1)S(1)}, u32[]{:S(2)}, u32[]{:S(2)}) collective-permute-start(bf16[64,2048]{1,0:T(8,128)(2,1)S(1)} %copy-done.108), channel_id=1, source_target_pairs={{0,3},{1,0},{2,1},{3,2},{4,7},{5,4},{6,5},{7,6},{8,11},{9,8},{10,9... | collective-permute-start | bytes 786440 | tf_op jit(solution)/shard_map/ppermute | solution.py:719
  114.6 111.1 %all-gather.10.cloned.1.call-start = ((), (), s32[]{:S(2)}) async-start(), calls=%async_computation.4 | async-start | bytes 9437184 | tf_op jit(solution)/shard_map/all_gather | solution.py:343
  115.2 360.4 %reduce-scatter.3.cloned.1.call-start = ((), (), s32[]{:S(2)}) async-start(), calls=%async_computation.5 | async-start | bytes 2359296 | tf_op jit(solution)/shard_map/reduce_scatter | solution.py:696
  127.2 16.0 %collective-permute-start.10 = (bf16[128,2048]{1,0:T(8,128)(2,1)S(1)}, bf16[128,2048]{1,0:T(8,128)(2,1)S(1)}, u32[]{:S(2)}, u32[]{:S(2)}) collective-permute-start(bf16[128,2048]{1,0:T(8,128)(2,1)S(1)} %convolution_convert_fusion.1), channel_id=1, source_target_pairs={{0,1},{1,2},{2,3},{3,0},{4,5},{5,6},{6,7},{7,4},{8,9},{9,10},{10,1... | collective-permute-start | bytes 1572872 | tf_op jit(solution)/shard_map/ppermute | solution.py:97
  143.3 15.2 %collective-permute-start.11 = (bf16[128,2048]{1,0:T(8,128)(2,1)S(1)}, bf16[128,2048]{1,0:T(8,128)(2,1)S(1)}, u32[]{:S(2)}, u32[]{:S(2)}) collective-permute-start(bf16[128,2048]{1,0:T(8,128)(2,1)S(1)} %add_convert_fusion.16), channel_id=1, source_target_pairs={{0,1},{1,2},{2,3},{3,0},{4,5},{5,6},{6,7},{7,4},{8,9},{9,10},{10,1... | collective-permute-start | bytes 1572872 | tf_op jit(solution)/shard_map/ppermute | solution.py:97
  159.4 14.6 %collective-permute-start.12 = (bf16[128,2048]{1,0:T(8,128)(2,1)}, bf16[128,2048]{1,0:T(8,128)(2,1)S(1)}, u32[]{:S(2)}, u32[]{:S(2)}) collective-permute-start(bf16[128,2048]{1,0:T(8,128)(2,1)} %add_convert_fusion.15), channel_id=1, source_target_pairs={{0,1},{1,2},{2,3},{3,0},{4,5},{5,6},{6,7},{7,4},{8,9},{9,10},{10,1... | collective-permute-start | bytes 1572872 | tf_op jit(solution)/shard_map/ppermute | solution.py:97
  175.5 13.3 %collective-permute-start.13 = (bf16[128,2048]{1,0:T(8,128)(2,1)S(1)}, bf16[128,2048]{1,0:T(8,128)(2,1)S(1)}, u32[]{:S(2)}, u32[]{:S(2)}) collective-permute-start(bf16[128,2048]{1,0:T(8,128)(2,1)S(1)} %add_convert_fusion.14.left_ref.refs_0_), channel_id=1, source_target_pairs={{0,1},{1,2},{2,3},{3,0},{4,5},{5,6},{6,7},{7,4},{8,9},{9,10},{10,1... | collective-permute-start | bytes 1572872 | tf_op jit(solution)/shard_map/ppermute | solution.py:77
  188.8 12.4 %collective-permute-start.14 = (bf16[128,2048]{1,0:T(8,128)(2,1)S(1)}, bf16[128,2048]{1,0:T(8,128)(2,1)S(1)}, u32[]{:S(2)}, u32[]{:S(2)}) collective-permute-start(bf16[128,2048]{1,0:T(8,128)(2,1)S(1)} %collective-permute-done.13.left_ref.refs_1_), channel_id=1, source_target_pairs={{0,1},{1,2},{2,3},{3,0},{4,5},{5,6},{6,7},{7,4},{8,9},{9,10},{10,1... | collective-permute-start | bytes 1572872 | tf_op jit(solution)/shard_map/ppermute | solution.py:77
  201.2 11.9 %collective-permute-start.15 = (bf16[128,2048]{1,0:T(8,128)(2,1)S(1)}, bf16[128,2048]{1,0:T(8,128)(2,1)S(1)}, u32[]{:S(2)}, u32[]{:S(2)}) collective-permute-start(bf16[128,2048]{1,0:T(8,128)(2,1)S(1)} %collective-permute-done.14.left_ref.refs_2_), channel_id=1, source_target_pairs={{0,1},{1,2},{2,3},{3,0},{4,5},{5,6},{6,7},{7,4},{8,9},{9,10},{10,1... | collective-permute-start | bytes 1572872 | tf_op jit(solution)/shard_map/ppermute | solution.py:77
  213.0 12.7 %collective-permute-start.16 = (bf16[128,2048]{1,0:T(8,128)(2,1)}, bf16[128,2048]{1,0:T(8,128)(2,1)}, u32[]{:S(2)}, u32[]{:S(2)}) collective-permute-start(bf16[128,2048]{1,0:T(8,128)(2,1)} %bitcast.40), channel_id=1, source_target_pairs={{0,1},{1,2},{2,3},{3,0},{4,5},{5,6},{6,7},{7,4},{8,9},{9,10},{10,1... | collective-permute-start | bytes 1572872 | tf_op jit(solution)/shard_map/ppermute | solution.py:106
  225.7 15.6 %collective-permute-start.18 = (bf16[128,2048]{1,0:T(8,128)(2,1)}, bf16[128,2048]{1,0:T(8,128)(2,1)}, u32[]{:S(2)}, u32[]{:S(2)}) collective-permute-start(bf16[128,2048]{1,0:T(8,128)(2,1)} %collective-permute-done.16), channel_id=1, source_target_pairs={{0,1},{1,2},{2,3},{3,0},{4,5},{5,6},{6,7},{7,4},{8,9},{9,10},{10,1... | collective-permute-start | bytes 1572872 | tf_op jit(solution)/shard_map/ppermute | solution.py:106
  241.5 16.6 %collective-permute-start.22 = (bf16[128,2048]{1,0:T(8,128)(2,1)}, bf16[128,2048]{1,0:T(8,128)(2,1)S(1)}, u32[]{:S(2)}, u32[]{:S(2)}) collective-permute-start(bf16[128,2048]{1,0:T(8,128)(2,1)} %collective-permute-done.18), channel_id=1, source_target_pairs={{0,1},{1,2},{2,3},{3,0},{4,5},{5,6},{6,7},{7,4},{8,9},{9,10},{10,1... | collective-permute-start | bytes 1572872 | tf_op jit(solution)/shard_map/ppermute | solution.py:106
  242.7 14.8 %collective-permute-start.19 = (f32[4,128]{1,0:T(4,128)S(1)}, f32[4,128]{1,0:T(4,128)S(1)}, u32[]{:S(2)}, u32[]{:S(2)}) collective-permute-start(f32[4,128]{1,0:T(4,128)S(1)} %pad_maximum_fusion.10), channel_id=1, source_target_pairs={{0,1},{1,2},{2,3},{3,0},{4,5},{5,6},{6,7},{7,4},{8,9},{9,10},{10,1... | collective-permute-start | bytes 6152 | tf_op jit(solution)/shard_map/ppermute | solution.py:763
  244.2 13.2 %collective-permute-start.20 = (f32[4,128]{1,0:T(4,128)S(1)}, f32[4,128]{1,0:T(4,128)S(1)}, u32[]{:S(2)}, u32[]{:S(2)}) collective-permute-start(f32[4,128]{1,0:T(4,128)S(1)} %pad_maximum_fusion.10), channel_id=1, source_target_pairs={{0,2},{1,3},{2,0},{3,1},{4,6},{5,7},{6,4},{7,5},{8,10},{9,11},{10,... | collective-permute-start | bytes 6152 | tf_op jit(solution)/shard_map/ppermute | solution.py:763
  246.1 11.3 %collective-permute-start.21 = (f32[4,128]{1,0:T(4,128)S(1)}, f32[4,128]{1,0:T(4,128)S(1)}, u32[]{:S(2)}, u32[]{:S(2)}) collective-permute-start(f32[4,128]{1,0:T(4,128)S(1)} %pad_maximum_fusion.10), channel_id=1, source_target_pairs={{0,3},{1,0},{2,1},{3,2},{4,7},{5,4},{6,5},{7,6},{8,11},{9,8},{10,9... | collective-permute-start | bytes 6152 | tf_op jit(solution)/shard_map/ppermute | solution.py:763
  275.3 14.6 %collective-permute-start.23 = (bf16[128,2048]{1,0:T(8,128)(2,1)S(1)}, bf16[128,2048]{1,0:T(8,128)(2,1)S(1)}, u32[]{:S(2)}, u32[]{:S(2)}) collective-permute-start(bf16[128,2048]{1,0:T(8,128)(2,1)S(1)} %convert_element_type.302), channel_id=1, source_target_pairs={{0,1},{1,2},{2,3},{3,0},{4,5},{5,6},{6,7},{7,4},{8,9},{9,10},{10,1... | collective-permute-start | bytes 1572872 | tf_op jit(solution)/shard_map/ppermute | solution.py:97
  290.8 16.2 %collective-permute-start.24 = (bf16[128,2048]{1,0:T(8,128)(2,1)}, bf16[128,2048]{1,0:T(8,128)(2,1)}, u32[]{:S(2)}, u32[]{:S(2)}) collective-permute-start(bf16[128,2048]{1,0:T(8,128)(2,1)} %add_convert_fusion.11), channel_id=1, source_target_pairs={{0,1},{1,2},{2,3},{3,0},{4,5},{5,6},{6,7},{7,4},{8,9},{9,10},{10,1... | collective-permute-start | bytes 1572872 | tf_op jit(solution)/shard_map/ppermute | solution.py:97
  320.7 36.2 %collective-permute-start.27 = (bf16[1024,2048]{1,0:T(8,128)(2,1)}, bf16[1024,2048]{1,0:T(8,128)(2,1)}, u32[]{:S(2)}, u32[]{:S(2)}) collective-permute-start(bf16[1024,2048]{1,0:T(8,128)(2,1)} %pair_product.4), channel_id=1, source_target_pairs={{0,4},{4,0},{8,12},{12,8},{16,20},{20,16},{24,28},{28,24},{1,5},{5... | collective-permute-start | bytes 12582920 | tf_op jit(solution)/shard_map/ppermute | solution.py:347
  320.7 16.4 %collective-permute-start.25 = (bf16[128,2048]{1,0:T(8,128)(2,1)S(1)}, bf16[128,2048]{1,0:T(8,128)(2,1)S(1)}, u32[]{:S(2)}, u32[]{:S(2)}) collective-permute-start(bf16[128,2048]{1,0:T(8,128)(2,1)S(1)} %add_convert_fusion.9), channel_id=1, source_target_pairs={{0,1},{1,2},{2,3},{3,0},{4,5},{5,6},{6,7},{7,4},{8,9},{9,10},{10,1... | collective-permute-start | bytes 1572872 | tf_op jit(solution)/shard_map/ppermute | solution.py:97
  340.8 16.1 %collective-permute-start.26 = (bf16[128,2048]{1,0:T(8,128)(2,1)}, bf16[128,2048]{1,0:T(8,128)(2,1)}, u32[]{:S(2)}, u32[]{:S(2)}) collective-permute-start(bf16[128,2048]{1,0:T(8,128)(2,1)} %get-tuple-element.194), channel_id=1, source_target_pairs={{0,1},{1,2},{2,3},{3,0},{4,5},{5,6},{6,7},{7,4},{8,9},{9,10},{10,1... | collective-permute-start | bytes 1572872 | tf_op jit(solution)/shard_map/ppermute | solution.py:77
  356.9 15.0 %collective-permute-start.28 = (bf16[128,2048]{1,0:T(8,128)(2,1)}, bf16[128,2048]{1,0:T(8,128)(2,1)}, u32[]{:S(2)}, u32[]{:S(2)}) collective-permute-start(bf16[128,2048]{1,0:T(8,128)(2,1)} %collective-permute-done.26), channel_id=1, source_target_pairs={{0,1},{1,2},{2,3},{3,0},{4,5},{5,6},{6,7},{7,4},{8,9},{9,10},{10,1... | collective-permute-start | bytes 1572872 | tf_op jit(solution)/shard_map/ppermute | solution.py:77
  368.4 13.2 %collective-permute-start.30 = (bf16[256,1024]{1,0:T(8,128)(2,1)}, bf16[256,1024]{1,0:T(8,128)(2,1)}, u32[]{:S(2)}, u32[]{:S(2)}) collective-permute-start(bf16[256,1024]{1,0:T(8,128)(2,1)} %get-tuple-element.200), channel_id=1, source_target_pairs={{0,8},{4,12},{8,0},{12,4},{16,24},{20,28},{24,16},{28,20},{1,9},{5... | collective-permute-start | bytes 1572872 | tf_op jit(solution)/shard_map/ppermute | solution.py:347
  369.9 12.9 %collective-permute-start.31 = (bf16[256,1024]{1,0:T(8,128)(2,1)}, bf16[256,1024]{1,0:T(8,128)(2,1)}, u32[]{:S(2)}, u32[]{:S(2)}) collective-permute-start(bf16[256,1024]{1,0:T(8,128)(2,1)} %get-tuple-element.204), channel_id=1, source_target_pairs={{0,16},{4,20},{8,24},{12,28},{16,0},{20,4},{24,8},{28,12},{1,17},{... | collective-permute-start | bytes 1572872 | tf_op jit(solution)/shard_map/ppermute | solution.py:347
  371.9 14.0 %collective-permute-start.29 = (bf16[128,2048]{1,0:T(8,128)(2,1)}, bf16[128,2048]{1,0:T(8,128)(2,1)S(1)}, u32[]{:S(2)}, u32[]{:S(2)}) collective-permute-start(bf16[128,2048]{1,0:T(8,128)(2,1)} %collective-permute-done.28), channel_id=1, source_target_pairs={{0,1},{1,2},{2,3},{3,0},{4,5},{5,6},{6,7},{7,4},{8,9},{9,10},{10,1... | collective-permute-start | bytes 1572872 | tf_op jit(solution)/shard_map/ppermute | solution.py:77
  389.9 182.3 %reduce-scatter.5.cloned.1.call-start = ((), (), s32[]{:S(2)}) async-start(), calls=%async_computation.6 | async-start | bytes 9437184 | tf_op jit(solution)/shard_map/reduce_scatter | solution.py:696
  391.2 13.0 %collective-permute-start.17 = (bf16[128,2048]{1,0:T(8,128)(2,1)S(1)}, bf16[128,2048]{1,0:T(8,128)(2,1)}, u32[]{:S(2)}, u32[]{:S(2)}) collective-permute-start(bf16[128,2048]{1,0:T(8,128)(2,1)S(1)} %slice.403), channel_id=1, source_target_pairs={{0,1},{1,2},{2,3},{3,0},{4,5},{5,6},{6,7},{7,4},{8,9},{9,10},{10,1... | collective-permute-start | bytes 1572872 | tf_op jit(solution)/shard_map/ppermute | solution.py:114
  417.4 46.7 %collective-permute-start.35 = (bf16[1024,1536]{1,0:T(8,128)(2,1)}, bf16[1024,1536]{1,0:T(8,128)(2,1)}, u32[]{:S(2)}, u32[]{:S(2)}) collective-permute-start(bf16[1024,1536]{1,0:T(8,128)(2,1)} %pair_product.6), channel_id=1, source_target_pairs={{0,4},{4,0},{8,12},{12,8},{16,20},{20,16},{24,28},{28,24},{1,5},{5... | collective-permute-start | bytes 9437192 | tf_op jit(solution)/shard_map/ppermute | solution.py:347
  418.5 31.6 %collective-permute-start.36 = (bf16[256,1024]{1,0:T(8,128)(2,1)}, bf16[256,1024]{1,0:T(8,128)(2,1)S(1)}, u32[]{:S(2)}, u32[]{:S(2)}) collective-permute-start(bf16[256,1024]{1,0:T(8,128)(2,1)} %get-tuple-element.198), channel_id=1, source_target_pairs={{0,8},{4,12},{8,0},{12,4},{16,24},{20,28},{24,16},{28,20},{1,9},{5... | collective-permute-start | bytes 1572872 | tf_op jit(solution)/shard_map/ppermute | solution.py:347
  419.9 36.1 %collective-permute-start.37 = (bf16[256,1024]{1,0:T(8,128)(2,1)}, bf16[256,1024]{1,0:T(8,128)(2,1)S(1)}, u32[]{:S(2)}, u32[]{:S(2)}) collective-permute-start(bf16[256,1024]{1,0:T(8,128)(2,1)} %get-tuple-element.203), channel_id=1, source_target_pairs={{0,16},{4,20},{8,24},{12,28},{16,0},{20,4},{24,8},{28,12},{1,17},{... | collective-permute-start | bytes 1572872 | tf_op jit(solution)/shard_map/ppermute | solution.py:347
  421.6 15.7 %collective-permute-start.32 = (bf16[128,2048]{1,0:T(8,128)(2,1)S(1)}, bf16[128,2048]{1,0:T(8,128)(2,1)S(1)}, u32[]{:S(2)}, u32[]{:S(2)}) collective-permute-start(bf16[128,2048]{1,0:T(8,128)(2,1)S(1)} %add_convert_fusion.8), channel_id=1, source_target_pairs={{0,1},{1,2},{2,3},{3,0},{4,5},{5,6},{6,7},{7,4},{8,9},{9,10},{10,1... | collective-permute-start | bytes 1572872 | tf_op jit(solution)/shard_map/ppermute | solution.py:114
  422.9 42.1 %collective-permute-start.39 = (bf16[256,1024]{1,0:T(8,128)(2,1)S(1)}, bf16[256,1024]{1,0:T(8,128)(2,1)S(1)}, u32[]{:S(2)}, u32[]{:S(2)}) collective-permute-start(bf16[256,1024]{1,0:T(8,128)(2,1)S(1)} %add_convert_fusion.5), channel_id=1, source_target_pairs={{0,16},{4,20},{8,24},{12,28},{16,0},{20,4},{24,8},{28,12},{1,17},{... | collective-permute-start | bytes 1572872 | tf_op jit(solution)/shard_map/ppermute | solution.py:347
  447.4 16.7 %collective-permute-start.34 = (bf16[128,2048]{1,0:T(8,128)(2,1)S(1)}, bf16[128,2048]{1,0:T(8,128)(2,1)S(1)}, u32[]{:S(2)}, u32[]{:S(2)}) collective-permute-start(bf16[128,2048]{1,0:T(8,128)(2,1)S(1)} %convert_element_type.332), channel_id=1, source_target_pairs={{0,1},{1,2},{2,3},{3,0},{4,5},{5,6},{6,7},{7,4},{8,9},{9,10},{10,1... | collective-permute-start | bytes 1572872 | tf_op jit(solution)/shard_map/ppermute | solution.py:97
  450.0 16.3 %collective-permute-start.40 = (bf16[256,1024]{1,0:T(8,128)(2,1)S(1)}, bf16[256,1024]{1,0:T(8,128)(2,1)S(1)}, u32[]{:S(2)}, u32[]{:S(2)}) collective-permute-start(bf16[256,1024]{1,0:T(8,128)(2,1)S(1)} %add_convert_fusion.4), channel_id=1, source_target_pairs={{0,8},{4,12},{8,0},{12,4},{16,24},{20,28},{24,16},{28,20},{1,9},{5... | collective-permute-start | bytes 1572872 | tf_op jit(solution)/shard_map/ppermute | solution.py:347
  456.1 61.6 %collective-permute-start.33 = (bf16[128,2048]{1,0:T(8,128)(2,1)}, bf16[128,2048]{1,0:T(8,128)(2,1)}, u32[]{:S(2)}, u32[]{:S(2)}) collective-permute-start(bf16[128,2048]{1,0:T(8,128)(2,1)} %add_convert_fusion.7), channel_id=1, source_target_pairs={{0,1},{1,2},{2,3},{3,0},{4,5},{5,6},{6,7},{7,4},{8,9},{9,10},{10,1... | collective-permute-start | bytes 1572872 | tf_op jit(solution)/shard_map/ppermute | solution.py:114
  465.0 23.6 %collective-permute-start.38 = (bf16[128,2048]{1,0:T(8,128)(2,1)}, bf16[128,2048]{1,0:T(8,128)(2,1)}, u32[]{:S(2)}, u32[]{:S(2)}) collective-permute-start(bf16[128,2048]{1,0:T(8,128)(2,1)} %add_convert_fusion.6), channel_id=1, source_target_pairs={{0,1},{1,2},{2,3},{3,0},{4,5},{5,6},{6,7},{7,4},{8,9},{9,10},{10,1... | collective-permute-start | bytes 1572872 | tf_op jit(solution)/shard_map/ppermute | solution.py:97
  473.3 23.6 %collective-permute-start.42 = (bf16[256,768]{1,0:T(8,128)(2,1)}, bf16[256,768]{1,0:T(8,128)(2,1)}, u32[]{:S(2)}, u32[]{:S(2)}) collective-permute-start(bf16[256,768]{1,0:T(8,128)(2,1)} %get-tuple-element.227), channel_id=1, source_target_pairs={{0,8},{4,12},{8,0},{12,4},{16,24},{20,28},{24,16},{28,20},{1,9},{5... | collective-permute-start | bytes 1179656 | tf_op jit(solution)/shard_map/ppermute | solution.py:347
  475.6 26.9 %collective-permute-start.43 = (bf16[256,768]{1,0:T(8,128)(2,1)}, bf16[256,768]{1,0:T(8,128)(2,1)}, u32[]{:S(2)}, u32[]{:S(2)}) collective-permute-start(bf16[256,768]{1,0:T(8,128)(2,1)} %get-tuple-element.231), channel_id=1, source_target_pairs={{0,16},{4,20},{8,24},{12,28},{16,0},{20,4},{24,8},{28,12},{1,17},{... | collective-permute-start | bytes 1179656 | tf_op jit(solution)/shard_map/ppermute | solution.py:347
  475.6 19.2 %collective-permute-start.59 = (bf16[64,2048]{1,0:T(8,128)(2,1)}, bf16[64,2048]{1,0:T(8,128)(2,1)}, u32[]{:S(2)}, u32[]{:S(2)}) collective-permute-start(bf16[64,2048]{1,0:T(8,128)(2,1)} %reduce-scatter.3.cloned.1.call-done), channel_id=1, source_target_pairs={{0,0},{16,1},{2,2},{18,3},{4,4},{20,5},{6,6},{22,7},{8,8},{24,9},{... | collective-permute-start | bytes 786440 | tf_op jit(solution)/shard_map/ppermute | solution.py:1033
  494.3 5.1 collective-permute-start.44
  494.9 38.7 %collective-permute-start.52 = (bf16[256,768]{1,0:T(8,128)(2,1)}, bf16[256,768]{1,0:T(8,128)(2,1)S(1)}, u32[]{:S(2)}, u32[]{:S(2)}) collective-permute-start(bf16[256,768]{1,0:T(8,128)(2,1)} %get-tuple-element.225), channel_id=1, source_target_pairs={{0,8},{4,12},{8,0},{12,4},{16,24},{20,28},{24,16},{28,20},{1,9},{5... | collective-permute-start | bytes 1179656 | tf_op jit(solution)/shard_map/ppermute | solution.py:347
  496.9 36.8 %collective-permute-start.54 = (bf16[256,768]{1,0:T(8,128)(2,1)}, bf16[256,768]{1,0:T(8,128)(2,1)S(1)}, u32[]{:S(2)}, u32[]{:S(2)}) collective-permute-start(bf16[256,768]{1,0:T(8,128)(2,1)} %get-tuple-element.230), channel_id=1, source_target_pairs={{0,16},{4,20},{8,24},{12,28},{16,0},{20,4},{24,8},{28,12},{1,17},{... | collective-permute-start | bytes 1179656 | tf_op jit(solution)/shard_map/ppermute | solution.py:347
  499.4 4.2 collective-permute-start.45
  502.5 13.2 %collective-permute-start.41 = (bf16[128,2048]{1,0:T(8,128)(2,1)S(1)}, bf16[128,2048]{1,0:T(8,128)(2,1)S(1)}, u32[]{:S(2)}, u32[]{:S(2)}) collective-permute-start(bf16[128,2048]{1,0:T(8,128)(2,1)S(1)} %add_convert_fusion.3), channel_id=1, source_target_pairs={{0,1},{1,2},{2,3},{3,0},{4,5},{5,6},{6,7},{7,4},{8,9},{9,10},{10,1... | collective-permute-start | bytes 1572872 | tf_op jit(solution)/shard_map/ppermute | solution.py:97
  504.9 19.3 %collective-permute-start.53 = (bf16[256,768]{1,0:T(8,128)(2,1)S(1)}, bf16[256,768]{1,0:T(8,128)(2,1)S(1)}, u32[]{:S(2)}, u32[]{:S(2)}) collective-permute-start(bf16[256,768]{1,0:T(8,128)(2,1)S(1)} %add_convert_fusion.24), channel_id=1, source_target_pairs={{0,16},{4,20},{8,24},{12,28},{16,0},{20,4},{24,8},{28,12},{1,17},{... | collective-permute-start | bytes 1179656 | tf_op jit(solution)/shard_map/ppermute | solution.py:347
  515.7 14.6 %collective-permute-start.55 = (bf16[256,768]{1,0:T(8,128)(2,1)S(1)}, bf16[256,768]{1,0:T(8,128)(2,1)S(1)}, u32[]{:S(2)}, u32[]{:S(2)}) collective-permute-start(bf16[256,768]{1,0:T(8,128)(2,1)S(1)} %add_convert_fusion.22), channel_id=1, source_target_pairs={{0,8},{4,12},{8,0},{12,4},{16,24},{20,28},{24,16},{28,20},{1,9},{5... | collective-permute-start | bytes 1179656 | tf_op jit(solution)/shard_map/ppermute | solution.py:347
  517.7 16.2 %collective-permute-start.47 = (bf16[64,2048]{1,0:T(8,128)(2,1)S(1)}, bf16[64,2048]{1,0:T(8,128)(2,1)S(1)}, u32[]{:S(2)}, u32[]{:S(2)}) collective-permute-start(bf16[64,2048]{1,0:T(8,128)(2,1)S(1)} %get-tuple-element.285), channel_id=1, source_target_pairs={{0,1},{1,2},{2,3},{3,0},{4,5},{5,6},{6,7},{7,4},{8,9},{9,10},{10,1... | collective-permute-start | bytes 786440 | tf_op jit(solution)/shard_map/ppermute | solution.py:719
  524.2 17.9 %collective-permute-start.48 = (bf16[64,2048]{1,0:T(8,128)(2,1)S(1)}, bf16[64,2048]{1,0:T(8,128)(2,1)S(1)}, u32[]{:S(2)}, u32[]{:S(2)}) collective-permute-start(bf16[64,2048]{1,0:T(8,128)(2,1)S(1)} %get-tuple-element.284), channel_id=1, source_target_pairs={{0,2},{1,3},{2,0},{3,1},{4,6},{5,7},{6,4},{7,5},{8,10},{9,11},{10,... | collective-permute-start | bytes 786440 | tf_op jit(solution)/shard_map/ppermute | solution.py:719
  530.3 12.1 %collective-permute-start.49 = (bf16[64,2048]{1,0:T(8,128)(2,1)S(1)}, bf16[64,2048]{1,0:T(8,128)(2,1)S(1)}, u32[]{:S(2)}, u32[]{:S(2)}) collective-permute-start(bf16[64,2048]{1,0:T(8,128)(2,1)S(1)} %get-tuple-element.283), channel_id=1, source_target_pairs={{0,3},{1,0},{2,1},{3,2},{4,7},{5,4},{6,5},{7,6},{8,11},{9,8},{10,9... | collective-permute-start | bytes 786440 | tf_op jit(solution)/shard_map/ppermute | solution.py:719
  542.4 5.9 %collective-permute-start.50 = (f32[2,832]{1,0:T(2,128)S(1)}, f32[2,832]{1,0:T(2,128)S(1)}, u32[]{:S(2)}, u32[]{:S(2)}) collective-permute-start(f32[2,832]{1,0:T(2,128)S(1)} %slice.315), channel_id=1, source_target_pairs={{0,2},{1,3},{2,0},{3,1},{4,6},{5,7},{6,4},{7,5},{8,10},{9,11},{10,... | collective-permute-start | bytes 19976 | tf_op jit(solution)/shard_map/ppermute | solution.py:347
  548.3 13.5 %collective-permute-start.51 = (f32[1,832]{1,0:T(1,128)S(1)}, f32[1,832]{1,0:T(1,128)S(1)}, u32[]{:S(2)}, u32[]{:S(2)}) collective-permute-start(f32[1,832]{1,0:T(1,128)S(1)} %slice.372), channel_id=1, source_target_pairs={{0,1},{1,0},{2,3},{3,2},{4,5},{5,4},{6,7},{7,6},{8,9},{9,8},{10,11... | collective-permute-start | bytes 9992 | tf_op jit(solution)/shard_map/ppermute | solution.py:347
  553.3 10.3 %collective-permute-start.56 = (bf16[64,1536]{1,0:T(8,128)(2,1)S(1)}, bf16[64,1536]{1,0:T(8,128)(2,1)S(1)}, u32[]{:S(2)}, u32[]{:S(2)}) collective-permute-start(bf16[64,1536]{1,0:T(8,128)(2,1)S(1)} %get-tuple-element.289), channel_id=1, source_target_pairs={{0,1},{1,2},{2,3},{3,0},{4,5},{5,6},{6,7},{7,4},{8,9},{9,10},{10,1... | collective-permute-start | bytes 589832 | tf_op jit(solution)/shard_map/ppermute | solution.py:719
  553.3 15.5 %collective-permute-start.57 = (bf16[64,1536]{1,0:T(8,128)(2,1)S(1)}, bf16[64,1536]{1,0:T(8,128)(2,1)S(1)}, u32[]{:S(2)}, u32[]{:S(2)}) collective-permute-start(bf16[64,1536]{1,0:T(8,128)(2,1)S(1)} %get-tuple-element.288), channel_id=1, source_target_pairs={{0,2},{1,3},{2,0},{3,1},{4,6},{5,7},{6,4},{7,5},{8,10},{9,11},{10,... | collective-permute-start | bytes 589832 | tf_op jit(solution)/shard_map/ppermute | solution.py:719
  556.2 12.6 %collective-permute-start.58 = (bf16[64,1536]{1,0:T(8,128)(2,1)S(1)}, bf16[64,1536]{1,0:T(8,128)(2,1)S(1)}, u32[]{:S(2)}, u32[]{:S(2)}) collective-permute-start(bf16[64,1536]{1,0:T(8,128)(2,1)S(1)} %get-tuple-element.287), channel_id=1, source_target_pairs={{0,3},{1,0},{2,1},{3,2},{4,7},{5,4},{6,5},{7,6},{8,11},{9,8},{10,9... | collective-permute-start | bytes 589832 | tf_op jit(solution)/shard_map/ppermute | solution.py:719
  (122 other events, 901.9 us)
Sparse Core Ops, SparseCore 0:
  10.5 38.4 all-gather.11
  51.4 47.7 all-gather.5
  114.7 54.3 all-gather.7
  170.9 54.3 all-gather.9
  390.0 41.4 reduce-scatter.2
  435.2 95.1 reduce-scatter.4
